TPU v7x, 32 devices: a whole 2x2x4 slice. The times are simulated.
32 devices in a mesh: dp: 8 (over z, x), frame: 4 (over y, core).
Axes of the slice: x: 2, y: 2, z: 4, core: 2. Of those that a mesh axis runs over, the one named last changes fastest.
Arguments:
- hidden_in: bfloat16 [8192, 1280], P(('dp', 'frame')), may hold values from -6 to 6
- rec_lengths: int32 [8, 3], P('dp'), may hold values from 1 to 512, 1024 in all within a row
- token_positions: int32 [8192], P('dp'), may hold values from 0 to 1535, as said below
- thinker_grad: bfloat16 [12288, 1280], P(('dp', 'frame')), may hold values from -6 to 6
- norm_gain: float32 [1280], replicated, may hold values from 0.25 to 1.75
- norm_bias: float32 [1280], replicated, may hold values from -3 to 3
- qkv_weight: bfloat16 [1280, 3, 1280], P('dp', None, 'frame'), may hold values from -10 to 10
Outputs:
- hidden_grad: bfloat16 [8192, 1280], P(('dp', 'frame'))
- weight_grad: float32 [1280, 3, 1280], P('dp', None, 'frame')
Inputs may be any that keep to these rules, and one draw needn't show every extreme that they name: `token_positions`: within each block of 1024 entries the positions increase strictly; the first is 0 and the last is 1535.
All inputs are finite; a program needn't handle non-finite values.
Results may differ from a plain program's by a relative error of at most 0.025.
The roundings to bfloat16 on the way count: a program that leaves them out, or rounds other values in their place, can miss the bound.
Values may be sent and summed in bfloat16 or wider, within the bound.
A program may use at most 128 MiB of HBM per device.

v0:
```python
import math

import jax
import jax.numpy as jnp
from jax import lax
from jax.sharding import PartitionSpec as P

HD = 64


norm_eps = 1e-05


def norm_forward(rows, gain, bias):
    rows_f32 = rows.astype(jnp.float32)
    mean_row = jnp.mean(rows_f32, axis=-1, keepdims=True)
    centered = rows_f32 - mean_row
    variance = jnp.mean(centered * centered, axis=-1, keepdims=True)
    inv_std = lax.rsqrt(variance + norm_eps)
    standard = centered * inv_std
    normalized = (standard * gain + bias).astype(jnp.bfloat16)
    return (normalized, standard, inv_std)


def norm_backward(norm_grad, standard, inv_std, gain):
    scaled = norm_grad * gain
    result = inv_std * (
        scaled
        - jnp.mean(scaled, axis=-1, keepdims=True)
        - standard * jnp.mean(scaled * standard, axis=-1, keepdims=True)
    )
    return result.astype(jnp.bfloat16)


def segment_ids(lengths, count):
    ends = jnp.cumsum(lengths)
    frame_ids = jnp.arange(count, dtype=jnp.int32)
    return jnp.sum((frame_ids[:, None] >= ends[None, :]).astype(jnp.int32), axis=1)


def head_pass(queries, keys_in, values, out_grad, segments, score_scale, block_rows):
    length = queries.shape[0]
    head_size = queries.shape[1]

    def step(totals, first_row):
        key_total, value_total = totals
        query_rows = lax.dynamic_slice_in_dim(queries, first_row, block_rows, 0)
        grad_rows = lax.dynamic_slice_in_dim(out_grad, first_row, block_rows, 0)
        seg_rows = lax.dynamic_slice_in_dim(segments, first_row, block_rows, 0)
        scores = jnp.einsum("qd,kd->qk", query_rows, keys_in, preferred_element_type=jnp.float32)
        same_rec = seg_rows[:, None] == segments[None, :]
        scores = jnp.where(same_rec, scores * score_scale, -1e30)
        row_max = jnp.max(scores, axis=-1, keepdims=True)
        expo = jnp.where(same_rec, jnp.exp(scores - row_max), 0.0)
        attn_weights = expo / jnp.sum(expo, axis=-1, keepdims=True)
        weight_grads = jnp.einsum(
            "qd,kd->qk", grad_rows, values, preferred_element_type=jnp.float32
        )
        row_dot = jnp.sum(attn_weights * weight_grads, axis=-1, keepdims=True)
        score_grad = (attn_weights * (weight_grads - row_dot)).astype(jnp.bfloat16)
        weights_low = attn_weights.astype(jnp.bfloat16)
        value_total = value_total + jnp.einsum(
            "qk,qd->kd", weights_low, grad_rows, preferred_element_type=jnp.float32
        )
        key_total = key_total + jnp.einsum(
            "qk,qd->kd", score_grad, query_rows, preferred_element_type=jnp.float32
        )
        query_grad = jnp.einsum(
            "qk,kd->qd", score_grad, keys_in, preferred_element_type=jnp.float32
        )
        return ((key_total, value_total), (query_grad * score_scale).astype(jnp.bfloat16))

    starts = jnp.arange(length // block_rows, dtype=jnp.int32) * block_rows
    zero_acc = jnp.zeros((length, head_size), jnp.float32)
    (key_total, value_total), query_grad = lax.scan(step, (zero_acc, zero_acc), starts)
    query_grad = query_grad.reshape(length, head_size)
    return (
        query_grad,
        (key_total * score_scale).astype(jnp.bfloat16),
        value_total.astype(jnp.bfloat16),
    )


def attention_grads(projected, out_grad, segments):
    length = projected.shape[0]
    head_cols = projected.shape[2]
    local_heads = head_cols // HD
    block_rows = math.gcd(length, 512)
    score_scale = HD ** (-0.5)

    def split_heads(block):
        return jnp.transpose(block.reshape(length, local_heads, HD), (1, 0, 2))

    def one_head(items):
        return head_pass(items[0], items[1], items[2], items[3], segments, score_scale, block_rows)

    grads = lax.map(
        one_head,
        (
            split_heads(projected[:, 0]),
            split_heads(projected[:, 1]),
            split_heads(projected[:, 2]),
            split_heads(out_grad),
        ),
    )
    merged = [jnp.transpose(item, (1, 0, 2)).reshape(length, head_cols) for item in grads]
    return jnp.stack(merged, axis=1)


def per_device(
    hidden_in, rec_lengths, token_positions, thinker_grad, norm_gain, norm_bias, qkv_weight
):
    frame_count = lax.axis_size("frame")
    width = hidden_in.shape[1]
    head_cols = qkv_weight.shape[2]
    group_frames = token_positions.shape[0]
    think_rows = thinker_grad.shape[0]
    normalized, standard, inv_std = norm_forward(hidden_in, norm_gain, norm_bias)
    segments = segment_ids(rec_lengths[0], group_frames)
    moved = lax.all_to_all(
        thinker_grad.reshape(think_rows, frame_count, head_cols),
        "frame",
        split_axis=1,
        concat_axis=0,
        tiled=True,
    )
    moved = moved.reshape(frame_count * think_rows, head_cols)
    out_grad = jnp.take(moved, token_positions, axis=0)
    group_norm = lax.all_gather(normalized, "frame", axis=0, tiled=True)
    column_weight = lax.all_gather(qkv_weight, "dp", axis=0, tiled=True)
    weight_flat = column_weight.reshape(width, 3 * head_cols)
    projected = jnp.dot(group_norm, weight_flat, preferred_element_type=jnp.float32)
    projected = projected.astype(jnp.bfloat16).reshape(group_frames, 3, head_cols)
    proj_grad = attention_grads(projected, out_grad, segments)
    grad_flat = proj_grad.reshape(group_frames, 3 * head_cols)
    norm_grad = lax.psum_scatter(
        lax.dot_general(
            grad_flat, weight_flat, (((1,), (1,)), ((), ())), preferred_element_type=jnp.float32
        ).astype(jnp.bfloat16),
        "frame",
        scatter_dimension=0,
        tiled=True,
    ).astype(jnp.float32)
    weight_part = lax.dot_general(
        group_norm, grad_flat, (((0,), (0,)), ((), ())), preferred_element_type=jnp.float32
    )
    weight_grad = lax.psum_scatter(
        weight_part.reshape(width, 3, head_cols).astype(jnp.bfloat16),
        "dp",
        scatter_dimension=0,
        tiled=True,
    ).astype(jnp.float32)
    hidden_grad = norm_backward(norm_grad, standard, inv_std, norm_gain)
    return (hidden_grad, weight_grad)


def solution(mesh):
    placed = (
        P(("dp", "frame"), None),
        P("dp", None),
        P("dp"),
        P(("dp", "frame"), None),
        P(),
        P(),
        P("dp", None, "frame"),
    )
    return jax.shard_map(
        per_device,
        mesh=mesh,
        in_specs=placed,
        out_specs=(P(("dp", "frame"), None), P("dp", None, "frame")),
        check_vma=False,
    )
```

profile of v0, /device:TPU:0, one launch (start us, length us, event | category | flops | bytes accessed | tf_op | source)
XLA Modules:
  0.0 394.7 jit_solution(15514916091266970238)
XLA Ops:
  14.5 4.2 %all-to-all-start = ((bf16[384,4,320]{0,2,1:T(8,128)(2,1)}), bf16[384,4,320]{0,2,1:T(8,128)(2,1)S(1)}, u32[]{:S(2)}, u32[]{:S(2)}) async-start(bf16[384,4,320]{0,2,1:T(8,128)(2,1)} %bitcast.11), calls=%async_computation | async-start | bytes 1966080 | tf_op jit(solution)/shard_map/all_to_all | solution.py:120
  19.1 13.4 %all-to-all-done = bf16[384,4,320]{0,2,1:T(8,128)(2,1)S(1)} async-done(((bf16[384,4,320]{0,2,1:T(8,128)(2,1)}), bf16[384,4,320]{0,2,1:T(8,128)(2,1)S(1)}, u32[]{:S(2)}, u32[]{:S(2)}) %all-to-all-start) | async-done | bytes 983072 | tf_op jit(solution)/shard_map/all_to_all | solution.py:120
  33.3 3.9 gather_fusion
  38.4 33.0 %all-gather.5.cloned.1.call-done = bf16[1280,3,320]{2,0,1:T(8,128)(2,1)} async-done(((bf16[160,3,320]{2,0,1:T(8,128)(2,1)}), bf16[1280,3,320]{2,0,1:T(8,128)(2,1)}) %all-gather.5.cloned.1.call-update) | async-done | bytes 2457616 | tf_op jit(solution)/shard_map/all_gather | solution.py:130
  71.4 3.9 copy.30
  75.3 21.9 %all-gather.3.cloned.1.call-done = bf16[1024,1280]{1,0:T(8,128)(2,1)} async-done(((bf16[256,1280]{1,0:T(8,128)(2,1)}), bf16[1024,1280]{1,0:T(8,128)(2,1)}) %all-gather.3.cloned.1.call-update) | async-done | bytes 2621456 | tf_op jit(solution)/shard_map/all_gather | solution.py:129
  97.2 4.5 %convolution_convert_fusion.1 = bf16[1024,960]{0,1:T(8,128)(2,1)S(1)} fusion(bf16[1024,1280]{1,0:T(8,128)(2,1)} %all-gather.3.cloned.1.call-done, bf16[1280,960]{0,1:T(8,128)(2,1)S(1)} %bitcast.98), kind=kOutput, calls=%fused_computation.40 | convolution fusion | flops 2517565440 | bytes 7045120 | tf_op jit(solution)/shard_map/dot_general | solution.py:132
  103.1 162.3 %while.30 = (s32[]{:T(128)}, bf16[5,1024,64]{2,1,0:T(8,128)(2,1)}, bf16[5,1024,64]{1,2,0:T(8,128)(2,1)}, bf16[5,1024,64]{1,2,0:T(8,128)(2,1)}, bf16[5,1024,64]{1...) while((s32[]{:T(128)}, bf16[5,1024,64]{2,1,0:T(8,128)(2,1)}, ...), condition=%wide.region_10.11_spmd, body=%wide.region_4.10_spmd.sunk | while | flops 347601408 | bytes 25794008 | solution.py:97
  109.5 23.4 %while.31 = (s32[]{:T(128)}, f32[1024,64]{0,1:T(8,128)}, f32[1024,64]{0,1:T(8,128)}, bf16[2,512,64]{1,2,0:T(8,128)(2,1)S(1)}, s32[2]{0:T(128)S(1)}, /*index=5*/s...) while((s32[]{:T(128)}, f32[1024,64]{0,1:T(8,128)}, ...), condition=%wide.region_9.9_spmd.clone, body=%wide.region_5.8_spmd.clone.sunk | while | flops 347404800 | bytes 22253772 | solution.py:75
  126.0 2.0 multiply_reduce_fusion.2
  128.3 2.1 convolution_add_fusion.4
  130.8 2.1 convolution_add_fusion.5
  142.0 23.4 %while.31 = (s32[]{:T(128)}, f32[1024,64]{0,1:T(8,128)}, f32[1024,64]{0,1:T(8,128)}, bf16[2,512,64]{1,2,0:T(8,128)(2,1)S(1)}, s32[2]{0:T(128)S(1)}, /*index=5*/s...) while((s32[]{:T(128)}, f32[1024,64]{0,1:T(8,128)}, ...), condition=%wide.region_9.9_spmd.clone, body=%wide.region_5.8_spmd.clone.sunk | while | flops 347404800 | bytes 22253772 | solution.py:75
  158.5 2.0 multiply_reduce_fusion.2
  160.8 2.1 convolution_add_fusion.4
  163.3 2.1 convolution_add_fusion.5
  174.4 23.4 %while.31 = (s32[]{:T(128)}, f32[1024,64]{0,1:T(8,128)}, f32[1024,64]{0,1:T(8,128)}, bf16[2,512,64]{1,2,0:T(8,128)(2,1)S(1)}, s32[2]{0:T(128)S(1)}, /*index=5*/s...) while((s32[]{:T(128)}, f32[1024,64]{0,1:T(8,128)}, ...), condition=%wide.region_9.9_spmd.clone, body=%wide.region_5.8_spmd.clone.sunk | while | flops 347404800 | bytes 22253772 | solution.py:75
  179.4 2.0 multiply_reduce_fusion.2
  193.2 2.1 convolution_add_fusion.4
  195.8 2.1 convolution_add_fusion.5
  206.9 23.4 %while.31 = (s32[]{:T(128)}, f32[1024,64]{0,1:T(8,128)}, f32[1024,64]{0,1:T(8,128)}, bf16[2,512,64]{1,2,0:T(8,128)(2,1)S(1)}, s32[2]{0:T(128)S(1)}, /*index=5*/s...) while((s32[]{:T(128)}, f32[1024,64]{0,1:T(8,128)}, ...), condition=%wide.region_9.9_spmd.clone, body=%wide.region_5.8_spmd.clone.sunk | while | flops 347404800 | bytes 22253772 | solution.py:75
  225.7 2.1 convolution_add_fusion.4
  228.2 2.1 convolution_add_fusion.5
  239.4 23.4 %while.31 = (s32[]{:T(128)}, f32[1024,64]{0,1:T(8,128)}, f32[1024,64]{0,1:T(8,128)}, bf16[2,512,64]{1,2,0:T(8,128)(2,1)S(1)}, s32[2]{0:T(128)S(1)}, /*index=5*/s...) while((s32[]{:T(128)}, f32[1024,64]{0,1:T(8,128)}, ...), condition=%wide.region_9.9_spmd.clone, body=%wide.region_5.8_spmd.clone.sunk | while | flops 347404800 | bytes 22253772 | solution.py:75
  255.9 2.0 multiply_reduce_fusion.2
  258.2 2.1 convolution_add_fusion.4
  260.7 2.1 convolution_add_fusion.5
  267.9 7.3 %convolution_convert_fusion = bf16[1280,3,320]{2,0,1:T(8,128)(2,1)} fusion(bf16[1024,1280]{1,0:T(8,128)(2,1)} %all-gather.3.cloned.1.call-done, bf16[1024,1,320]{0,2,1:T(8,128)(2,1)} %bitcast.106, bf16[1024,1,320]{0,2,1:T(8,128)(2,1)} %bitcast.104, bf16[1024,1,320]{0,2,1:T(8,128)(2,1)S(1)} %bitcast.101), kind=kOutput, calls=%fused_computation.36 | convolution fusion | flops 2523709440 | bytes 7045120 | tf_op jit(solution)/shard_map/dot_general | solution.py:144
  277.1 6.7 %bitcast_convert_fusion = bf16[1024,1280]{1,0:T(8,128)(2,1)} fusion(bf16[1280,3,320]{2,0,1:T(8,128)(2,1)S(1)} %copy-done.2, bf16[1024,1,320]{0,2,1:T(8,128)(2,1)} %bitcast.107, bf16[1024,1,320]{0,2,1:T(8,128)(2,1)} %bitcast.105, bf16[1024,1,320]{0,2,1:T(8,128)(2,1)} %bitcast.102), kind=kOutput, calls=%fused_computation.35 | convolution fusion | flops 2519859200 | bytes 7045120 | tf_op jit(solution)/shard_map/dot_general | solution.py:137
  283.8 64.0 %reduce-scatter.5.cloned.1.call-done = bf16[160,3,320]{2,0,1:T(8,128)(2,1)} async-done(((bf16[1280,3,320]{2,0,1:T(8,128)(2,1)}), bf16[160,3,320]{2,0,1:T(8,128)(2,1)}) %reduce-scatter.5.cloned.1.call-update) | async-done | bytes 307216 | tf_op jit(solution)/shard_map/reduce_scatter | solution.py:147
  349.7 34.4 %reduce-scatter.3.cloned.1.call-done = bf16[256,1280]{1,0:T(8,128)(2,1)} async-done(((bf16[1024,1280]{1,0:T(8,128)(2,1)}), bf16[256,1280]{1,0:T(8,128)(2,1)}) %reduce-scatter.3.cloned.1.call-update) | async-done | bytes 655376 | tf_op jit(solution)/shard_map/reduce_scatter | solution.py:136
  385.7 2.4 fusion.31
  (204 shorter events, 131.2 us)
Async XLA Ops:
  7.2 4.1 %copy-start = (bf16[256,1280]{1,0:T(8,128)(2,1)S(1)}, bf16[256,1280]{1,0:T(8,128)(2,1)}, u32[]{:S(2)}) copy-start(bf16[256,1280]{1,0:T(8,128)(2,1)} %param.11) | copy-start | bytes 1966084
  7.2 6.0 %copy-start.3 = (bf16[384,1280]{1,0:T(8,128)(2,1)S(1)}, bf16[384,1280]{1,0:T(8,128)(2,1)}, u32[]{:S(2)}) copy-start(bf16[384,1280]{1,0:T(8,128)(2,1)} %param.14) | copy-start | bytes 2949124
  7.2 64.2 %all-gather.5.cloned.1.call-start = ((), (), s32[]{:S(2)}) async-start(), calls=%async_computation.4 | async-start | bytes 3317760 | tf_op jit(solution)/shard_map/all_gather | solution.py:130
  7.9 89.2 %all-gather.3.cloned.1.call-start = ((), (), s32[]{:S(2)}) async-start(), calls=%async_computation.3 | async-start | bytes 3276800 | tf_op jit(solution)/shard_map/all_gather | solution.py:129
  9.2 5.3 %copy-start.6 = (f32[256]{0:T(256)}, f32[256]{0:T(256)S(1)}, u32[]{:S(2)}) copy-start(f32[256]{0:T(256)S(1)} %broadcast_multiply_fusion.2) | copy-start | bytes 3076
  10.7 0.6 copy-start.9
  13.2 5.6 %copy-start.11 = (s32[1,3]{1,0:T(1,128)S(1)}, s32[1,3]{1,0:T(1,128)}, u32[]{:S(2)}) copy-start(s32[1,3]{1,0:T(1,128)} %param.12) | copy-start | bytes 40
  13.2 5.9 %copy-start.8 = (s32[1024]{0:T(1024)S(1)}, s32[1024]{0:T(1024)}, u32[]{:S(2)}) copy-start(s32[1024]{0:T(1024)} %param.13) | copy-start | bytes 12292
  14.5 18.0 %all-to-all-start = ((bf16[384,4,320]{0,2,1:T(8,128)(2,1)}), bf16[384,4,320]{0,2,1:T(8,128)(2,1)S(1)}, u32[]{:S(2)}, u32[]{:S(2)}) async-start(bf16[384,4,320]{0,2,1:T(8,128)(2,1)} %bitcast.11), calls=%async_computation | async-start | bytes 1966080 | tf_op jit(solution)/shard_map/all_to_all | solution.py:120
  18.8 329.1 %reduce-scatter.5.cloned.1.call-start = ((), (), s32[]{:S(2)}) async-start(), calls=%async_computation.6 | async-start | bytes 3317760 | tf_op jit(solution)/shard_map/reduce_scatter | solution.py:147
  267.0 0.9 copy-start.4
  275.2 1.8 copy-start.2
  275.3 108.9 %reduce-scatter.3.cloned.1.call-start = ((), (), s32[]{:S(2)}) async-start(), calls=%async_computation.5 | async-start | bytes 3276800 | tf_op jit(solution)/shard_map/reduce_scatter | solution.py:136
  283.8 100.4 %copy-start.1 = (bf16[256,1280]{1,0:T(8,128)(2,1)S(1)}, bf16[256,1280]{1,0:T(8,128)(2,1)}, u32[]{:S(2)}) copy-start(bf16[256,1280]{1,0:T(8,128)(2,1)} %param.11) | copy-start | bytes 1966084
  283.8 100.4 %copy-start.5 = (f32[1280]{0:T(1024)S(1)}, f32[1280]{0:T(1024)}, u32[]{:S(2)}) copy-start(f32[1280]{0:T(1024)} %param.15) | copy-start | bytes 15364
  283.8 100.4 %copy-start.7 = (f32[256]{0:T(256)S(1)}, f32[256]{0:T(256)}, u32[]{:S(2)}) copy-start(f32[256]{0:T(256)} %copy-done.6) | copy-start | bytes 3076
  283.8 100.4 %copy-start.10 = (f32[256]{0:T(256)S(1)}, f32[256]{0:T(256)}, u32[]{:S(2)}) copy-start(f32[256]{0:T(256)} %copy-done.9) | copy-start | bytes 3076
Sparse Core Ops, SparseCore 0:
  10.2 61.1 all-gather.4
  72.9 24.1 all-gather.2
  275.4 72.4 reduce-scatter.4
  350.4 33.7 reduce-scatter.2
where the time goes:
time: 397 us; the launch traced here: 395 us
  waiting for transfers between devices  167 us (42%)
  matrix products  97.8 us (25%)
  local copies, waits for them, and re-layouts  59.9 us (15%)
  other arithmetic  30 us (8%)
  loops' own time  21 us (5%)
  between operations  13.9 us (4%)
  starting transfers between devices  4.54 us (1%)
    reduce_scatter x1, waiting for transfers between devices, per_device(): lax.psum_scatter(weight_part.reshape(width, 3, head_cols).astype(jnp.bflo...  64 us
    reduce_scatter x1, waiting for transfers between devices, per_device(): lax.psum_scatter(lax.dot_general(grad_flat, weight_flat, (((1,), (1,)), (...  34.4 us
    all_gather x1, waiting for transfers between devices, per_device(): column_weight = lax.all_gather(qkv_weight, 'dp', axis=0, tiled=True)  33 us
    dynamic_slice x40, local copies, waits for them, and re-layouts, attention_grads(): lax.map(one_head, (split_heads(projected[:, 0]), split_heads(projected[:,...  31.7 us
    all_gather x1, waiting for transfers between devices, per_device(): group_norm = lax.all_gather(normalized, 'frame', axis=0, tiled=True)  21.9 us
    another operation x5, loops' own time, head_pass(): lax.scan(step, (zero_acc, zero_acc), starts)  20.9 us
    dot_general x10, matrix products, step(): jnp.einsum('qk,qd->kd', weights_low, grad_rows, preferred_element_type=jn...  20.3 us
    dot_general x10, matrix products, step(): jnp.einsum('qk,qd->kd', score_grad, query_rows, preferred_element_type=jn...  20.3 us
  transfers between devices with their start and end apart: 5, of which 5 were waited for; matrix products, arithmetic and copies ran while one was open for 6% of the time, Pallas kernels for 0%

commit v1 on v0

v1 whole, which is shorter than its diff:
```python
import functools
import math

import jax
import jax.numpy as jnp
from jax import lax
from jax.experimental import pallas as pl
from jax.experimental.pallas import tpu as pltpu
from jax.sharding import PartitionSpec as P

HD = 64
MESH = pl.DeviceIdType.MESH
VMEM_LIMIT = 56 * 1024 * 1024

norm_eps = 1e-05
NEG = -1e30


def norm_forward(rows, gain, bias):
    rows_f32 = rows.astype(jnp.float32)
    mean_row = jnp.mean(rows_f32, axis=-1, keepdims=True)
    centered = rows_f32 - mean_row
    variance = jnp.mean(centered * centered, axis=-1, keepdims=True)
    inv_std = lax.rsqrt(variance + norm_eps)
    standard = centered * inv_std
    normalized = (standard * gain + bias).astype(jnp.bfloat16)
    return (normalized, standard, inv_std)


def norm_backward(norm_grad, standard, inv_std, gain):
    scaled = norm_grad * gain
    result = inv_std * (
        scaled
        - jnp.mean(scaled, axis=-1, keepdims=True)
        - standard * jnp.mean(scaled * standard, axis=-1, keepdims=True)
    )
    return result.astype(jnp.bfloat16)


def gather_kernel(
    dp, frames, w_ref, n_ref, t_ref, wg_ref, ng_ref, tg_ref,
    w_send, w_recv, n_send, n_recv, t_send, t_recv, own_sem,
):
    line = dp // 2
    pairs = frames // 2
    i = lax.axis_index("dp")
    f = lax.axis_index("frame")
    x, p = lax.rem(i, 2), lax.div(i, 2)
    c, u = lax.rem(f, 2), lax.div(f, 2)
    mate = p * 2 + (1 - x)
    right, left = i + 2, i - 2
    has_right, has_left = p < line - 1, p > 0

    barrier = pltpu.get_barrier_semaphore()
    pl.semaphore_signal(barrier, inc=1, device_id=(mate, f), device_id_type=MESH)

    @pl.when(has_right)
    def _():
        pl.semaphore_signal(barrier, inc=1, device_id=(right, f), device_id_type=MESH)

    @pl.when(has_left)
    def _():
        pl.semaphore_signal(barrier, inc=1, device_id=(left, f), device_id_type=MESH)

    for step in range(1, frames):
        other = lax.rem(f + step, frames)
        pl.semaphore_signal(barrier, inc=1, device_id=(i, other), device_id_type=MESH)
    ends = jnp.where(has_right, 1, 0) + jnp.where(has_left, 1, 0)
    pl.semaphore_wait(barrier, frames + ends)

    def w_copy(src, slot, way, target):
        return pltpu.make_async_remote_copy(
            src_ref=src, dst_ref=wg_ref.at[slot],
            send_sem=w_send.at[way, slot], recv_sem=w_recv.at[slot],
            device_id=(target, f), device_id_type=MESH,
        )

    def n_copy(src, slot, way, target):
        return pltpu.make_async_remote_copy(
            src_ref=src, dst_ref=ng_ref.at[slot],
            send_sem=n_send.at[way, slot], recv_sem=n_recv.at[slot],
            device_id=(i, target), device_id_type=MESH,
        )

    def t_copy(target):
        return pltpu.make_async_remote_copy(
            src_ref=t_ref.at[target], dst_ref=tg_ref.at[f],
            send_sem=t_send.at[target], recv_sem=t_recv.at[f],
            device_id=(i, target), device_id_type=MESH,
        )

    @pl.when(has_right)
    def _():
        w_copy(w_ref, i, 0, right).start()

    @pl.when(has_left)
    def _():
        w_copy(w_ref, i, 1, left).start()

    w_copy(w_ref, i, 2, mate).start()
    sibling = u * 2 + (1 - c)
    for step in range(1, pairs):
        far = lax.rem(u + step, pairs) * 2 + c
        n_copy(n_ref, f, step, far).start()
    n_copy(n_ref, f, 0, sibling).start()
    for step in range(1, frames):
        t_copy(lax.rem(f + step, frames)).start()
    own_w = pltpu.make_async_copy(w_ref, wg_ref.at[i], own_sem.at[0])
    own_n = pltpu.make_async_copy(n_ref, ng_ref.at[f], own_sem.at[1])
    own_t = pltpu.make_async_copy(t_ref.at[f], tg_ref.at[f], own_sem.at[2])
    own_w.start()
    own_n.start()
    own_t.start()

    def relay(step):
        from_left = i - 2 * step
        from_right = i + 2 * step

        @pl.when(p - step >= 0)
        def _():
            w_copy(w_ref, from_left, 0, mate).wait_recv()

            @pl.when(has_right)
            def _():
                w_copy(wg_ref.at[from_left], from_left, 0, right).start()

            w_copy(wg_ref.at[from_left], from_left, 2, mate).start()

        @pl.when(p + step <= line - 1)
        def _():
            w_copy(w_ref, from_right, 1, mate).wait_recv()

            @pl.when(has_left)
            def _():
                w_copy(wg_ref.at[from_right], from_right, 1, left).start()

            w_copy(wg_ref.at[from_right], from_right, 2, mate).start()

    def relay_norm():
        for step in range(1, pairs):
            far = lax.rem(u + step, pairs) * 2 + c
            n_copy(n_ref, far, 0, sibling).wait_recv()
            n_copy(ng_ref.at[far], far, 0, sibling).start()

    for step in range(1, min(line, 3)):
        relay(step)
    relay_norm()
    if line > 3:
        lax.fori_loop(3, line, lambda s, z: (relay(s), z)[1], 0)

    def finish(q, z):
        w_copy(w_ref, q * 2 + (1 - x), 2, mate).wait_recv()
        w_copy(w_ref, q * 2 + x, 2, mate).wait_send()

        @pl.when(jnp.logical_and(q <= p, has_right))
        def _():
            w_copy(w_ref, q * 2 + x, 0, right).wait_send()

        @pl.when(jnp.logical_and(q >= p, has_left))
        def _():
            w_copy(w_ref, q * 2 + x, 1, left).wait_send()

        return z

    for step in range(1, pairs):
        far = lax.rem(u + step, pairs) * 2 + c
        n_copy(n_ref, f, step, far).wait_send()
        n_copy(n_ref, far, 0, sibling).wait_send()
    n_copy(n_ref, f, 0, sibling).wait_send()
    for v in range(pairs):
        n_copy(n_ref, v * 2 + (1 - c), 0, sibling).wait_recv()
    for step in range(1, frames):
        other = lax.rem(f + step, frames)
        t_copy(other).wait_send()
        pltpu.make_async_remote_copy(
            src_ref=t_ref.at[other], dst_ref=tg_ref.at[other],
            send_sem=t_send.at[other], recv_sem=t_recv.at[other],
            device_id=(i, other), device_id_type=MESH,
        ).wait_recv()
    lax.fori_loop(0, line, finish, 0)
    own_w.wait()
    own_n.wait()
    own_t.wait()


def gather_all(dp, frames, weight, normalized, thinker):
    dma = pltpu.SemaphoreType.DMA
    any_spec = pl.BlockSpec(memory_space=pl.ANY)
    pairs = frames // 2
    moved = 2 * (dp * weight.size + frames * normalized.size + thinker.size)
    return pl.pallas_call(
        functools.partial(gather_kernel, dp, frames),
        out_shape=(
            jax.ShapeDtypeStruct((dp,) + weight.shape, weight.dtype),
            jax.ShapeDtypeStruct((frames,) + normalized.shape, normalized.dtype),
            jax.ShapeDtypeStruct(thinker.shape, thinker.dtype),
        ),
        in_specs=[any_spec] * 3,
        out_specs=(any_spec,) * 3,
        scratch_shapes=[
            dma((3, dp)), dma((dp,)),
            dma((pairs, frames)), dma((frames,)),
            dma((frames,)), dma((frames,)),
            dma((3,)),
        ],
        compiler_params=pltpu.CompilerParams(
            collective_id=0, has_side_effects=True, vmem_limit_bytes=VMEM_LIMIT
        ),
        cost_estimate=pl.CostEstimate(flops=0, bytes_accessed=2 * moved, transcendentals=0),
        name="gather_all",
    )(weight, normalized, thinker)


def local_kernel(
    rows_tile, tile_q, windows, len_ref, pos_ref, n_ref, w_ref, t_ref, ng_ref, wp_ref,
    q_s, k_s, v_s, g_s, kt_s, dq_s, dk_s, dv_s, dk_acc, dv_acc, grad_s,
):
    length, width = n_ref.shape
    cols = w_ref.shape[1]
    heads = cols // (3 * HD)
    recs = len_ref.shape[1]
    slack = t_ref.shape[0] - length
    scale = HD ** (-0.5)
    expo_scale = scale * math.log2(math.e)

    ends = []
    total = 0
    for r in range(recs):
        total = total + len_ref[0, r]
        ends.append(total)

    @pl.loop(0, length // rows_tile)
    def _(t):
        r0 = pl.multiple_of(t * rows_tile, rows_tile)
        rows = pl.ds(r0, rows_tile)
        proj = jnp.dot(n_ref[rows, :], w_ref[...], preferred_element_type=jnp.float32)
        proj = proj.astype(jnp.bfloat16)
        frame_ids = r0 + lax.broadcasted_iota(jnp.int32, (rows_tile, HD), 0)
        lane = lax.broadcasted_iota(jnp.int32, (rows_tile, HD), 1)
        seg = jnp.zeros((rows_tile, HD), jnp.int32)
        for end in ends:
            seg = seg + jnp.where(frame_ids >= end, 1, 0)
        same = seg == lane
        q_mask = jnp.where(jnp.logical_or(same, lane >= recs), 0.0, NEG).astype(jnp.bfloat16)
        k_mask = jnp.where(same, 1.0, 0.0).astype(jnp.bfloat16)
        cover = rows_tile + slack
        col = r0 + lax.broadcasted_iota(jnp.int32, (rows_tile, cover), 1)
        pick = jnp.where(col == pos_ref[rows, :], 1.0, 0.0).astype(jnp.bfloat16)
        out_grad = jnp.dot(
            pick, t_ref[pl.ds(r0, cover), :], preferred_element_type=jnp.float32
        ).astype(jnp.bfloat16)
        for h in range(heads):
            base = 3 * HD * h
            keys = proj[:, base + HD:base + 2 * HD]
            q_s[h, rows, 0:HD] = proj[:, base:base + HD]
            q_s[h, rows, HD:2 * HD] = q_mask
            k_s[h, rows, 0:HD] = keys
            k_s[h, rows, HD:2 * HD] = k_mask
            kt_s[h, :, rows] = keys.T
            v_s[h, rows, :] = proj[:, base + 2 * HD:base + 3 * HD]
            g_s[h, rows, :] = out_grad[:, h * HD:(h + 1) * HD]

    tiles = length // tile_q
    nt = (((1,), (1,)), ((), ()))

    @pl.loop(0, heads)
    def _(h):
        dk_acc[...] = jnp.zeros_like(dk_acc)
        dv_acc[...] = jnp.zeros_like(dv_acc)

        @pl.loop(0, tiles)
        def _(t):
            q0 = pl.multiple_of(t * tile_q, tile_q)
            q_last = q0 + tile_q - 1
            low = jnp.int32(0)
            high = jnp.int32(length)
            for end in ends:
                low = jnp.where(end <= q0, jnp.maximum(low, end), low)
                high = jnp.where(end > q_last, jnp.minimum(high, end), high)
            low = (low // 128) * 128
            need = high - low

            def attend(window):
                start = pl.multiple_of(jnp.minimum(low, length - window), 128)
                span = pl.ds(start, window)
                q_rows = q_s[h, pl.ds(q0, tile_q), :]
                g_rows = g_s[h, pl.ds(q0, tile_q), :]
                scores = lax.dot_general(
                    k_s[h, span, :], q_rows, nt, preferred_element_type=jnp.float32
                )
                grads = lax.dot_general(
                    v_s[h, span, :], g_rows, nt, preferred_element_type=jnp.float32
                )
                top = jnp.max(scores, axis=0, keepdims=True)
                expo = jnp.exp2((scores - top) * expo_scale)
                weights = expo * (1.0 / jnp.sum(expo, axis=0, keepdims=True))
                row_dot = jnp.sum(weights * grads, axis=0, keepdims=True)
                score_grad = (weights * (grads - row_dot)).astype(jnp.bfloat16)
                dv_acc[span, :] += jnp.dot(
                    weights.astype(jnp.bfloat16), g_rows, preferred_element_type=jnp.float32
                )
                dk_acc[span, :] += jnp.dot(
                    score_grad, q_rows[:, 0:HD], preferred_element_type=jnp.float32
                )
                dq_t = jnp.dot(kt_s[h, :, span], score_grad, preferred_element_type=jnp.float32)
                dq_s[h, pl.ds(q0, tile_q), :] = (dq_t * scale).T.astype(jnp.bfloat16)

            smaller = 0
            for window in windows:
                @pl.when(jnp.logical_and(need > smaller, need <= window))
                def _(window=window):
                    attend(window)
                smaller = window

        dk_s[h] = (dk_acc[...] * scale).astype(jnp.bfloat16)
        dv_s[h] = dv_acc[...].astype(jnp.bfloat16)

    @pl.loop(0, length // rows_tile)
    def _(t):
        rows = pl.ds(pl.multiple_of(t * rows_tile, rows_tile), rows_tile)
        parts = []
        for h in range(heads):
            parts += [dq_s[h, rows, :], dk_s[h, rows, :], dv_s[h, rows, :]]
        grad = jnp.concatenate(parts, axis=1)
        grad_s[rows, :] = grad
        ng_ref[rows, :] = lax.dot_general(
            grad, w_ref[...], nt, preferred_element_type=jnp.float32
        ).astype(jnp.bfloat16)

    @pl.loop(0, width // rows_tile)
    def _(t):
        rows = pl.ds(pl.multiple_of(t * rows_tile, rows_tile), rows_tile)
        wp_ref[rows, :] = lax.dot_general(
            n_ref[:, rows], grad_s[...], (((0,), (0,)), ((), ())),
            preferred_element_type=jnp.float32,
        ).astype(jnp.bfloat16)


def local_work(lengths, positions, group_norm, weight, thinker):
    length, width = group_norm.shape
    cols = weight.shape[1]
    heads = cols // (3 * HD)
    rows_tile = 256
    tile_q = 256
    windows = tuple(w for w in (512, 768) if w < length) + (length,)
    vmem = pl.BlockSpec(memory_space=pltpu.VMEM)
    bf16, f32 = jnp.bfloat16, jnp.float32
    return pl.pallas_call(
        functools.partial(local_kernel, rows_tile, tile_q, windows),
        out_shape=(
            jax.ShapeDtypeStruct((length, width), bf16),
            jax.ShapeDtypeStruct((width, cols), bf16),
        ),
        in_specs=[pl.BlockSpec(memory_space=pltpu.SMEM)] + [vmem] * 4,
        out_specs=(vmem, vmem),
        scratch_shapes=[
            pltpu.VMEM((heads, length, 2 * HD), bf16),
            pltpu.VMEM((heads, length, 2 * HD), bf16),
            pltpu.VMEM((heads, length, HD), bf16),
            pltpu.VMEM((heads, length, HD), bf16),
            pltpu.VMEM((heads, HD, length), bf16),
            pltpu.VMEM((heads, length, HD), bf16),
            pltpu.VMEM((heads, length, HD), bf16),
            pltpu.VMEM((heads, length, HD), bf16),
            pltpu.VMEM((length, HD), f32),
            pltpu.VMEM((length, HD), f32),
            pltpu.VMEM((length, cols), bf16),
        ],
        compiler_params=pltpu.CompilerParams(vmem_limit_bytes=VMEM_LIMIT),
        name="local_work",
    )(lengths, positions, group_norm, weight, thinker)


def per_device(
    hidden_in, rec_lengths, token_positions, thinker_grad, norm_gain, norm_bias, qkv_weight
):
    frame_count = lax.axis_size("frame")
    dp_count = lax.axis_size("dp")
    own_rows, three, head_cols = qkv_weight.shape
    heads = head_cols // HD
    width = hidden_in.shape[1]
    group_frames = token_positions.shape[0]
    think_rows = thinker_grad.shape[0]
    normalized, standard, inv_std = norm_forward(hidden_in, norm_gain, norm_bias)
    by_head = qkv_weight.reshape(own_rows, 3, heads, HD).transpose(0, 2, 1, 3)
    by_head = by_head.reshape(own_rows, 3 * head_cols)
    by_target = thinker_grad.reshape(think_rows, frame_count, head_cols).transpose(1, 0, 2)
    weight, group_norm, moved = gather_all(dp_count, frame_count, by_head, normalized, by_target)
    norm_part, weight_part = local_work(
        rec_lengths,
        token_positions.reshape(group_frames, 1),
        group_norm.reshape(group_frames, width),
        weight.reshape(width, 3 * head_cols),
        moved.reshape(frame_count * think_rows, head_cols),
    )
    norm_grad = lax.psum_scatter(
        norm_part, "frame", scatter_dimension=0, tiled=True
    ).astype(jnp.float32)
    weight_grad = lax.psum_scatter(
        weight_part, "dp", scatter_dimension=0, tiled=True
    ).astype(jnp.float32)
    weight_grad = weight_grad.reshape(own_rows, heads, 3, HD).transpose(0, 2, 1, 3)
    weight_grad = weight_grad.reshape(own_rows, 3, head_cols)
    hidden_grad = norm_backward(norm_grad, standard, inv_std, norm_gain)
    return (hidden_grad, weight_grad)


def solution(mesh):
    placed = (
        P(("dp", "frame"), None),
        P("dp", None),
        P("dp"),
        P(("dp", "frame"), None),
        P(),
        P(),
        P("dp", None, "frame"),
    )
    return jax.shard_map(
        per_device,
        mesh=mesh,
        in_specs=placed,
        out_specs=(P(("dp", "frame"), None), P("dp", None, "frame")),
        check_vma=False,
    )
```

time: 397 us -> 215 us (0.54)
  matrix products: 97.8 us -> 0 us
  Pallas kernels: 0 us -> 79.5 us
  waiting for transfers between devices: 167 us -> 108 us
  local copies, waits for them, and re-layouts: 59.9 us -> 6.78 us
  other arithmetic: 30 us -> 6.76 us
  loops' own time: 21 us -> 0 us
  starting transfers between devices: 4.54 us -> 0.08 us
    dot_general x53 -> x0, matrix products: 97.8 us -> none  [the longest x10 20.3 us: step(): jnp.einsum('qk,qd->kd', weights_low, grad_rows, preferred_element_type=jn...]
    pallas_call x0 -> x2, Pallas kernels: none -> 79.5 us  [the longest x1 43.3 us: gather_all(): pl.pallas_call(functools.partial(gather_kernel, dp, frames), out_shape=(j...]
    all_gather x2 -> x0, waiting for transfers between devices: 54.8 us -> none  [the longest x1 33 us: per_device(): column_weight = lax.all_gather(qkv_weight, 'dp', axis=0, tiled=True)]
    dynamic_slice x60 -> x0, local copies, waits for them, and re-layouts: 39.1 us -> none  [the longest x40 31.7 us: attention_grads(): lax.map(one_head, (split_heads(projected[:, 0]), split_heads(projected[:,...]
    another operation x6 -> x0, loops' own time: 21 us -> none  [the longest x5 20.9 us: head_pass(): lax.scan(step, (zero_acc, zero_acc), starts)]
    all_to_all x1 -> x0, waiting for transfers between devices: 13.4 us -> none  [per_device(): lax.all_to_all(thinker_grad.reshape(think_rows, frame_count, head_cols),...]
    reduce_scatter x2, waiting for transfers between devices: 98.5 us -> 108 us  [the longest x1 74.1 us: per_device(): lax.psum_scatter(weight_part, 'dp', scatter_dimension=0, tiled=True)]
    dynamic_update_slice x5 -> x0, other arithmetic: 8.82 us -> none  [attention_grads(): lax.map(one_head, (split_heads(projected[:, 0]), split_heads(projected[:,...]
  transfers between devices with their start and end apart: 5 -> 2, of which waited for: 5 -> 2; matrix products, arithmetic and copies ran while one was open for 6% -> 1% of each run, Pallas kernels for 0% -> 0%
where the time goes in v1:
time: 215 us; the launch traced here: 216 us
  waiting for transfers between devices  108 us (50%)
  Pallas kernels  79.5 us (37%)
  between operations  14.2 us (7%)
  local copies, waits for them, and re-layouts  6.78 us (3%)
  other arithmetic  6.76 us (3%)
    reduce_scatter x1, waiting for transfers between devices, per_device(): lax.psum_scatter(weight_part, 'dp', scatter_dimension=0, tiled=True)  74.1 us
    pallas_call x1, Pallas kernels, gather_all(): pl.pallas_call(functools.partial(gather_kernel, dp, frames), out_shape=(j...  43.3 us
    pallas_call x1, Pallas kernels, local_work(): pl.pallas_call(functools.partial(local_kernel, rows_tile, tile_q, windows...  36.2 us
    reduce_scatter x1, waiting for transfers between devices, per_device(): lax.psum_scatter(norm_part, 'frame', scatter_dimension=0, tiled=True)  33.7 us
  transfers between devices with their start and end apart: 2, of which 2 were waited for; matrix products, arithmetic and copies ran while one was open for 1% of the time, Pallas kernels for 0%

profile of v1, /device:TPU:0, one launch (start us, length us, event | category | flops | bytes accessed | tf_op | source)
XLA Modules:
  0.0 215.7 jit_solution(8231761244932878934)
XLA Ops:
  7.2 0.0 copy-start.3
  7.2 0.0 reduce-scatter.5.cloned.1.call-start
  7.2 1.3 convert_reduce_fusion
  8.5 1.4 fusion.11
  9.9 0.0 copy-done.3
  9.9 0.0 copy-start.6
  10.0 0.2 copy.11
  10.2 0.0 copy-start.2
  10.2 0.9 copy.15.w_ref
  11.2 0.0 copy-done.6
  11.2 1.0 copy.16.pos_ref
  12.2 0.0 copy-done.2
  12.2 0.6 copy.13
  12.8 0.0 copy-start
  12.9 0.0 copy-start.4
  12.9 0.0 copy-start.5
  12.9 1.4 copy.14
  14.3 0.0 copy-done
  14.3 0.0 copy-done.4
  14.3 1.1 fusion.6.n_ref
  15.5 43.3 %gather_all.1 = (bf16[8,160,960]{2,1,0:T(8,128)(2,1)}, bf16[4,256,1280]{2,1,0:T(8,128)(2,1)}, bf16[4,384,320]{2,1,0:T(8,128)(2,1)}) custom-call(bf16[160,960]{1,0:T(8,128)(2,1)} %copy.15.w_ref, bf16[256,1280]{1,0:T(8,128)(2,1)} %fusion.6.n_ref, bf16[4,384,320]{2,1,0:T(8,128)(2,1)} %bitcast.14), custom_call_target="tpu_custom_call" | custom-call | bytes 12124160 | tf_op jit(solution)/shard_map/gather_all/pallas_call | solution.py:191
  58.8 36.2 %local_work.1 = (bf16[1024,1280]{1,0:T(8,128)(2,1)}, bf16[1280,960]{1,0:T(8,128)(2,1)}) custom-call(s32[1,3]{1,0:T(1,128)} %len_ref.1, s32[1024,1]{1,0:T(8,128)} %copy.16.pos_ref, bf16[1024,1280]{1,0:T(8,128)(2,1)} %bitcast.19, bf16[1280,960]{1,0:T(8,128)(2,1)} %bitcast.18, bf16[1536,320]{1,0:T(8,128)(2,1)} %bitcast.22), custom_call_target="tpu_custom_call" | custom-call | tf_op jit(solution)/shard_map/local_work/pallas_call | solution.py:348
  95.0 0.0 reduce-scatter.5.cloned.1.call-update
  95.0 0.0 reduce-scatter.3.cloned.1.call-start
  95.1 0.7 reduce-scatter.3.cloned.1.call-update
  95.8 74.1 %reduce-scatter.5.cloned.1.call-done = bf16[160,960]{1,0:T(8,128)(2,1)} async-done(((bf16[1280,960]{1,0:T(8,128)(2,1)}), bf16[160,960]{1,0:T(8,128)(2,1)}) %reduce-scatter.5.cloned.1.call-update) | async-done | bytes 307216 | tf_op jit(solution)/shard_map/reduce_scatter | solution.py:399
  169.8 1.2 copy.17
  171.0 0.1 copy.18
  171.1 1.2 copy.19
  172.3 33.7 %reduce-scatter.3.cloned.1.call-done = bf16[256,1280]{1,0:T(8,128)(2,1)} async-done(((bf16[1024,1280]{1,0:T(8,128)(2,1)}), bf16[256,1280]{1,0:T(8,128)(2,1)}) %reduce-scatter.3.cloned.1.call-update) | async-done | bytes 655376 | tf_op jit(solution)/shard_map/reduce_scatter | solution.py:396
  206.0 1.6 fusion.12
  207.6 1.3 fusion.10
  (7 shorter events, 0.1 us)
Async XLA Ops:
  7.2 2.8 %copy-start.3 = (bf16[160,3,320]{2,0,1:T(8,128)(2,1)S(1)}, bf16[160,3,320]{2,0,1:T(8,128)(2,1)}, u32[]{:S(2)}) copy-start(bf16[160,3,320]{2,0,1:T(8,128)(2,1)} %param.13) | copy-start | bytes 921604
  7.2 162.7 %reduce-scatter.5.cloned.1.call-start = ((), (), s32[]{:S(2)}) async-start(), calls=%async_computation.3 | async-start | bytes 2949120 | tf_op jit(solution)/shard_map/reduce_scatter | solution.py:399
  9.9 1.2 copy-start.6
  10.2 2.0 copy-start.2
  12.8 1.5 copy-start
  12.9 1.5 copy-start.4
  12.9 1.4 copy-start.5
  95.0 110.9 %reduce-scatter.3.cloned.1.call-start = ((), (), s32[]{:S(2)}) async-start(), calls=%async_computation.2 | async-start | bytes 3276800 | tf_op jit(solution)/shard_map/reduce_scatter | solution.py:396
  206.0 1.6 copy-start.1
Sparse Core Ops, SparseCore 0:
  95.1 74.6 reduce-scatter.4
  172.4 33.5 reduce-scatter.2

commit v2 on v1

--- a/solution.py
+++ b/solution.py
@@ -38,9 +38,10 @@
 
 
 def gather_kernel(
-    dp, frames, w_ref, n_ref, t_ref, wg_ref, ng_ref, tg_ref,
-    w_send, w_recv, n_send, n_recv, t_send, t_recv, own_sem,
+    dp, frames, w_in, h_in, gain_ref, bias_ref, t_in, wg_ref, ng_ref, tg_ref,
+    w_ref, n_ref, t_ref, w_send, w_recv, n_send, n_recv, t_send, t_recv, own_sem,
 ):
+    head_cols = w_in.shape[2]
     line = dp // 2
     pairs = frames // 2
     i = lax.axis_index("dp")
@@ -65,6 +66,11 @@
     for step in range(1, frames):
         other = lax.rem(f + step, frames)
         pl.semaphore_signal(barrier, inc=1, device_id=(i, other), device_id_type=MESH)
+    for h in range(head_cols // HD):
+        for kind in range(3):
+            at = (3 * h + kind) * HD
+            w_ref[:, at:at + HD] = w_in[kind, :, h * HD:(h + 1) * HD]
+
     ends = jnp.where(has_right, 1, 0) + jnp.where(has_left, 1, 0)
     pl.semaphore_wait(barrier, frames + ends)
 
@@ -99,10 +105,13 @@
 
     w_copy(w_ref, i, 2, mate).start()
     sibling = u * 2 + (1 - c)
+    n_ref[...] = norm_forward(h_in[...], gain_ref[...], bias_ref[...])[0]
     for step in range(1, pairs):
         far = lax.rem(u + step, pairs) * 2 + c
         n_copy(n_ref, f, step, far).start()
     n_copy(n_ref, f, 0, sibling).start()
+    for target in range(frames):
+        t_ref[target] = t_in[:, target * head_cols:(target + 1) * head_cols]
     for step in range(1, frames):
         t_copy(lax.rem(f + step, frames)).start()
     own_w = pltpu.make_async_copy(w_ref, wg_ref.at[i], own_sem.at[0])
@@ -183,21 +192,29 @@
     own_t.wait()
 
 
-def gather_all(dp, frames, weight, normalized, thinker):
+def gather_all(dp, frames, weight, hidden, gain, bias, thinker):
     dma = pltpu.SemaphoreType.DMA
     any_spec = pl.BlockSpec(memory_space=pl.ANY)
+    vmem = pl.BlockSpec(memory_space=pltpu.VMEM)
     pairs = frames // 2
-    moved = 2 * (dp * weight.size + frames * normalized.size + thinker.size)
+    kinds, own_rows, head_cols = weight.shape
+    think_rows = thinker.shape[0]
+    w_own = (own_rows, kinds * head_cols)
+    t_own = (frames, think_rows, head_cols)
+    moved = 2 * (dp * weight.size + frames * hidden.size + thinker.size)
     return pl.pallas_call(
         functools.partial(gather_kernel, dp, frames),
         out_shape=(
-            jax.ShapeDtypeStruct((dp,) + weight.shape, weight.dtype),
-            jax.ShapeDtypeStruct((frames,) + normalized.shape, normalized.dtype),
-            jax.ShapeDtypeStruct(thinker.shape, thinker.dtype),
+            jax.ShapeDtypeStruct((dp,) + w_own, weight.dtype),
+            jax.ShapeDtypeStruct((frames,) + hidden.shape, hidden.dtype),
+            jax.ShapeDtypeStruct(t_own, thinker.dtype),
         ),
-        in_specs=[any_spec] * 3,
+        in_specs=[vmem] * 5,
         out_specs=(any_spec,) * 3,
         scratch_shapes=[
+            pltpu.VMEM(w_own, weight.dtype),
+            pltpu.VMEM(hidden.shape, hidden.dtype),
+            pltpu.VMEM(t_own, thinker.dtype),
             dma((3, dp)), dma((dp,)),
             dma((pairs, frames)), dma((frames,)),
             dma((frames,)), dma((frames,)),
@@ -208,7 +225,7 @@
         ),
         cost_estimate=pl.CostEstimate(flops=0, bytes_accessed=2 * moved, transcendentals=0),
         name="gather_all",
-    )(weight, normalized, thinker)
+    )(weight, hidden, gain, bias, thinker)
 
 
 def local_kernel(
@@ -245,7 +262,8 @@
         k_mask = jnp.where(same, 1.0, 0.0).astype(jnp.bfloat16)
         cover = rows_tile + slack
         col = r0 + lax.broadcasted_iota(jnp.int32, (rows_tile, cover), 1)
-        pick = jnp.where(col == pos_ref[rows, :], 1.0, 0.0).astype(jnp.bfloat16)
+        places = jnp.broadcast_to(pos_ref[:, rows], (128, rows_tile)).T[:, 0:1]
+        pick = jnp.where(col == places, 1.0, 0.0).astype(jnp.bfloat16)
         out_grad = jnp.dot(
             pick, t_ref[pl.ds(r0, cover), :], preferred_element_type=jnp.float32
         ).astype(jnp.bfloat16)
@@ -371,6 +389,211 @@
     )(lengths, positions, group_norm, weight, thinker)
 
 
+def reduce_kernel(
+    dp, frames, wp_ref, np_ref, h_ref, gain_ref, wout_ref, hout_ref,
+    from_mate, from_line, to_line, from_sib, from_far, to_far,
+    m_send, m_recv, l_send, l_recv, s_send, s_recv, f_send, f_recv,
+):
+    line = dp // 2
+    pairs = frames // 2
+    i = lax.axis_index("dp")
+    f = lax.axis_index("frame")
+    x, p = lax.rem(i, 2), lax.div(i, 2)
+    c, u = lax.rem(f, 2), lax.div(f, 2)
+    mate = p * 2 + (1 - x)
+    right, left = i + 2, i - 2
+    has_right, has_left = p < line - 1, p > 0
+    sibling = u * 2 + (1 - c)
+    f32, bf16 = jnp.float32, jnp.bfloat16
+
+    barrier = pltpu.get_barrier_semaphore()
+    pl.semaphore_signal(barrier, inc=1, device_id=(mate, f), device_id_type=MESH)
+
+    @pl.when(has_right)
+    def _():
+        pl.semaphore_signal(barrier, inc=1, device_id=(right, f), device_id_type=MESH)
+
+    @pl.when(has_left)
+    def _():
+        pl.semaphore_signal(barrier, inc=1, device_id=(left, f), device_id_type=MESH)
+
+    pl.semaphore_signal(barrier, inc=1, device_id=(i, sibling), device_id_type=MESH)
+    for step in range(1, pairs):
+        far = lax.rem(u + step, pairs) * 2 + c
+        pl.semaphore_signal(barrier, inc=1, device_id=(i, far), device_id_type=MESH)
+    ends = jnp.where(has_right, 1, 0) + jnp.where(has_left, 1, 0)
+    pl.semaphore_wait(barrier, 1 + pairs + ends)
+
+    def to_mate(q):
+        return pltpu.make_async_remote_copy(
+            src_ref=wp_ref.at[q * 2 + (1 - x)], dst_ref=from_mate.at[q],
+            send_sem=m_send.at[q], recv_sem=m_recv.at[q],
+            device_id=(mate, f), device_id_type=MESH,
+        )
+
+    def along(q, way, target):
+        return pltpu.make_async_remote_copy(
+            src_ref=to_line.at[q], dst_ref=from_line.at[way, q],
+            send_sem=l_send.at[q], recv_sem=l_recv.at[way, q],
+            device_id=(target, f), device_id_type=MESH,
+        )
+
+    def to_sibling(v):
+        return pltpu.make_async_remote_copy(
+            src_ref=np_ref.at[v * 2 + (1 - c)], dst_ref=from_sib.at[v],
+            send_sem=s_send.at[v], recv_sem=s_recv.at[v],
+            device_id=(i, sibling), device_id_type=MESH,
+        )
+
+    def to_other(v, slot):
+        return pltpu.make_async_remote_copy(
+            src_ref=to_far.at[v], dst_ref=from_far.at[slot],
+            send_sem=f_send.at[v], recv_sem=f_recv.at[slot],
+            device_id=(i, v * 2 + c), device_id_type=MESH,
+        )
+
+    ahead, behind = line - 1 - p, p
+
+    def target_at(s):
+        lower = jnp.where(s < ahead, line - 1 - s, s - ahead)
+        upper = jnp.where(s < behind, s, line - 1 - (s - behind))
+        return jnp.where(p < line // 2, lower, upper)
+
+    for step in range(1, pairs):
+        to_sibling(lax.rem(u + step, pairs)).start()
+    lax.fori_loop(0, line, lambda s, z: (to_mate(target_at(s)).start(), z)[1], 0)
+    to_sibling(u).start()
+
+    for step in range(1, pairs):
+        v = lax.rem(u + step, pairs)
+        to_sibling(v).wait_recv()
+        to_far[v] = (np_ref[v * 2 + c].astype(f32) + from_sib[v].astype(f32)).astype(bf16)
+        to_other(v, u).start()
+
+    def pass_on(s, z):
+        q = target_at(s)
+        to_mate(q).wait_recv()
+
+        @pl.when(jnp.logical_and(q >= p, has_left))
+        def _():
+            along(q, 0, right).wait_recv()
+
+        @pl.when(jnp.logical_and(q <= p, has_right))
+        def _():
+            along(q, 1, left).wait_recv()
+
+        def own():
+            return wp_ref[q * 2 + x].astype(f32) + from_mate[q].astype(f32)
+
+        @pl.when(q > p)
+        def _():
+            @pl.when(has_left)
+            def _():
+                to_line[q] = (own() + from_line[0, q].astype(f32)).astype(bf16)
+
+            @pl.when(jnp.logical_not(has_left))
+            def _():
+                to_line[q] = own().astype(bf16)
+
+            along(q, 0, right).start()
+
+        @pl.when(q < p)
+        def _():
+            @pl.when(has_right)
+            def _():
+                to_line[q] = (own() + from_line[1, q].astype(f32)).astype(bf16)
+
+            @pl.when(jnp.logical_not(has_right))
+            def _():
+                to_line[q] = own().astype(bf16)
+
+            along(q, 1, left).start()
+
+        return z
+
+    lax.fori_loop(0, line - 1, pass_on, 0)
+
+    to_sibling(u).wait_recv()
+    total = np_ref[f].astype(f32) + from_sib[u].astype(f32)
+    for step in range(1, pairs):
+        v = lax.rem(u + step, pairs)
+        to_other(v, v).wait_recv()
+        total = total + from_far[v].astype(f32)
+    rows = h_ref[...].astype(f32)
+    mean_row = jnp.mean(rows, axis=-1, keepdims=True)
+    centered = rows - mean_row
+    inv_std = lax.rsqrt(jnp.mean(centered * centered, axis=-1, keepdims=True) + norm_eps)
+    hout_ref[...] = norm_backward(total, centered * inv_std, inv_std, gain_ref[...])
+
+    pass_on(line - 1, 0)
+    kinds, _, head_cols = wout_ref.shape
+    zero = jnp.zeros(wp_ref.shape[1:], f32)
+
+    @pl.when(jnp.logical_not(has_left))
+    def _():
+        from_line[0, p] = zero.astype(bf16)
+
+    @pl.when(jnp.logical_not(has_right))
+    def _():
+        from_line[1, p] = zero.astype(bf16)
+
+    final = wp_ref[i].astype(f32) + from_mate[p].astype(f32)
+    final = final + from_line[0, p].astype(f32) + from_line[1, p].astype(f32)
+    for h in range(head_cols // HD):
+        for kind in range(kinds):
+            at = (kinds * h + kind) * HD
+            wout_ref[kind, :, h * HD:(h + 1) * HD] = final[:, at:at + HD]
+
+    def sent(q, z):
+        to_mate(q).wait_send()
+
+        @pl.when(q != p)
+        def _():
+            along(q, 0, right).wait_send()
+
+        return z
+
+    lax.fori_loop(0, line, sent, 0)
+    for v in range(pairs):
+        to_sibling(v).wait_send()
+    for step in range(1, pairs):
+        v = lax.rem(u + step, pairs)
+        to_other(v, u).wait_send()
+
+
+def reduce_all(dp, frames, weight_part, norm_part, hidden, gain, heads):
+    dma = pltpu.SemaphoreType.DMA
+    vmem = pl.BlockSpec(memory_space=pltpu.VMEM)
+    pairs, line = frames // 2, dp // 2
+    bf16, f32 = jnp.bfloat16, jnp.float32
+    own_rows, cols = weight_part.shape[1:]
+    moved = 2 * (weight_part.size + norm_part.size)
+    return pl.pallas_call(
+        functools.partial(reduce_kernel, dp, frames),
+        out_shape=(
+            jax.ShapeDtypeStruct((3, own_rows, cols // 3), f32),
+            jax.ShapeDtypeStruct(hidden.shape, bf16),
+        ),
+        in_specs=[vmem] * 4,
+        out_specs=(vmem,) * 2,
+        scratch_shapes=[
+            pltpu.VMEM((line, own_rows, cols), bf16),
+            pltpu.VMEM((2, line, own_rows, cols), bf16),
+            pltpu.VMEM((line, own_rows, cols), bf16),
+            pltpu.VMEM((pairs,) + hidden.shape, bf16),
+            pltpu.VMEM((pairs,) + hidden.shape, bf16),
+            pltpu.VMEM((pairs,) + hidden.shape, bf16),
+            dma((line,)), dma((line,)), dma((line,)), dma((2, line)),
+            dma((pairs,)), dma((pairs,)), dma((pairs,)), dma((pairs,)),
+        ],
+        compiler_params=pltpu.CompilerParams(
+            collective_id=1, has_side_effects=True, vmem_limit_bytes=VMEM_LIMIT
+        ),
+        cost_estimate=pl.CostEstimate(flops=0, bytes_accessed=2 * moved, transcendentals=0),
+        name="reduce_all",
+    )(weight_part, norm_part, hidden, gain)
+
+
 def per_device(
     hidden_in, rec_lengths, token_positions, thinker_grad, norm_gain, norm_bias, qkv_weight
 ):
@@ -378,31 +601,28 @@
     dp_count = lax.axis_size("dp")
     own_rows, three, head_cols = qkv_weight.shape
     heads = head_cols // HD
-    width = hidden_in.shape[1]
+    own_frames, width = hidden_in.shape
     group_frames = token_positions.shape[0]
     think_rows = thinker_grad.shape[0]
-    normalized, standard, inv_std = norm_forward(hidden_in, norm_gain, norm_bias)
-    by_head = qkv_weight.reshape(own_rows, 3, heads, HD).transpose(0, 2, 1, 3)
-    by_head = by_head.reshape(own_rows, 3 * head_cols)
-    by_target = thinker_grad.reshape(think_rows, frame_count, head_cols).transpose(1, 0, 2)
-    weight, group_norm, moved = gather_all(dp_count, frame_count, by_head, normalized, by_target)
+    gain = norm_gain.reshape(1, width)
+    weight, group_norm, moved = gather_all(
+        dp_count, frame_count, qkv_weight.transpose(1, 0, 2), hidden_in,
+        gain, norm_bias.reshape(1, width), thinker_grad,
+    )
     norm_part, weight_part = local_work(
         rec_lengths,
-        token_positions.reshape(group_frames, 1),
+        token_positions.reshape(1, group_frames),
         group_norm.reshape(group_frames, width),
         weight.reshape(width, 3 * head_cols),
         moved.reshape(frame_count * think_rows, head_cols),
     )
-    norm_grad = lax.psum_scatter(
-        norm_part, "frame", scatter_dimension=0, tiled=True
-    ).astype(jnp.float32)
-    weight_grad = lax.psum_scatter(
-        weight_part, "dp", scatter_dimension=0, tiled=True
-    ).astype(jnp.float32)
-    weight_grad = weight_grad.reshape(own_rows, heads, 3, HD).transpose(0, 2, 1, 3)
-    weight_grad = weight_grad.reshape(own_rows, 3, head_cols)
-    hidden_grad = norm_backward(norm_grad, standard, inv_std, norm_gain)
-    return (hidden_grad, weight_grad)
+    weight_grad, hidden_grad = reduce_all(
+        dp_count, frame_count,
+        weight_part.reshape(dp_count, own_rows, 3 * head_cols),
+        norm_part.reshape(frame_count, own_frames, width),
+        hidden_in, gain, heads,
+    )
+    return (hidden_grad, weight_grad.transpose(1, 0, 2))
 
 
 def solution(mesh):

time: 215 us -> 121 us (0.56)
  waiting for transfers between devices: 108 us -> 0 us
  Pallas kernels: 79.5 us -> 114 us
  between operations: 14.2 us -> 0.65 us
  other arithmetic: 6.76 us -> 0 us
    reduce_scatter x2 -> x0, waiting for transfers between devices: 108 us -> none  [the longest x1 74.1 us: per_device(): lax.psum_scatter(weight_part, 'dp', scatter_dimension=0, tiled=True)]
    pallas_call x0 -> x1, Pallas kernels: none -> 36.6 us  [reduce_all(): pl.pallas_call(functools.partial(reduce_kernel, dp, frames), out_shape=(j...]
    reduce_sum x3 -> x0, other arithmetic: 4.28 us -> none  [the longest x1 1.58 us: norm_backward(): jnp.mean(scaled, axis=-1, keepdims=True)]
    convert_element_type x2 -> x0, other arithmetic: 2.46 us -> none  [the longest x1 1.31 us: norm_backward(): return result.astype(jnp.bfloat16)]
    pallas_call x1, Pallas kernels: 43.3 us -> 41 us  [gather_all(): pl.pallas_call(functools.partial(gather_kernel, dp, frames), out_shape=(j...]
    reshape x5 -> x2, local copies, waits for them, and re-layouts: 4.62 us -> 2.59 us  [the longest x1 1.29 us: per_device(): gain = norm_gain.reshape(1, width)]
  transfers between devices with their start and end apart: 2 -> 0, of which waited for: 2 -> 0; matrix products, arithmetic and copies ran while one was open for 1% -> 0% of each run, Pallas kernels for 0% -> 0%
where the time goes in v2:
time: 121 us
  Pallas kernels  114 us (94%)
  local copies, waits for them, and re-layouts  6.58 us (5%)
    pallas_call x1, Pallas kernels, gather_all(): pl.pallas_call(functools.partial(gather_kernel, dp, frames), out_shape=(j...  41 us
    pallas_call x1, Pallas kernels, reduce_all(): pl.pallas_call(functools.partial(reduce_kernel, dp, frames), out_shape=(j...  36.6 us
    pallas_call x1, Pallas kernels, local_work(): pl.pallas_call(functools.partial(local_kernel, rows_tile, tile_q, windows...  36.1 us
    unnamed x2, local copies, waits for them, and re-layouts  3.99 us

profile of v2, /device:TPU:0, one launch (start us, length us, event | category | flops | bytes accessed | tf_op | source)
XLA Modules:
  0.0 121.0 jit_solution(5063481310872809978)
XLA Ops:
  0.6 1.3 %reshape.29.gain_ref = f32[1,1280]{1,0:T(1,128)} reshape(f32[1280]{0:T(1024)} %param.11) | data formatting | bytes 10240 | tf_op jit(solution)/shard_map/reshape | solution.py:607
  1.9 1.3 %reshape.30.bias_ref = f32[1,1280]{1,0:T(1,128)} reshape(f32[1280]{0:T(1024)} %param.12) | data formatting | bytes 10240 | tf_op jit(solution)/shard_map/reshape | solution.py:610
  3.2 41.0 %gather_all.1 = (bf16[8,160,960]{2,1,0:T(8,128)(2,1)}, bf16[4,256,1280]{2,1,0:T(8,128)(2,1)}, bf16[4,384,320]{2,1,0:T(8,128)(2,1)}) custom-call(bf16[3,160,320]{2,1,0:T(8,128)(2,1)} %bitcast.14, bf16[256,1280]{1,0:T(8,128)(2,1)} %h_ref.1, f32[1,1280]{1,0:T(1,128)} %reshape.29.gain_ref, f32[1,1280]{1,0:T(1,128)} %reshape.30.bias_ref, bf16[384,1280]{1,0:T(8,128)(2,1)} %t_in.1), custom_call_target="tpu_custom_call" | custom-call | bytes 12124160 | tf_op jit(solution)/shard_map/gather_all/pallas_call | solution.py:205
  44.2 36.1 %local_work.1 = (bf16[1024,1280]{1,0:T(8,128)(2,1)}, bf16[1280,960]{1,0:T(8,128)(2,1)}) custom-call(s32[1,3]{1,0:T(1,128)} %len_ref.1, s32[1,1024]{1,0:T(1,128)} %bitcast.15, bf16[1024,1280]{1,0:T(8,128)(2,1)} %bitcast.11, bf16[1280,960]{1,0:T(8,128)(2,1)} %bitcast.10, bf16[1536,320]{1,0:T(8,128)(2,1)} %bitcast.12), custom_call_target="tpu_custom_call" | custom-call | tf_op jit(solution)/shard_map/local_work/pallas_call | solution.py:366
  80.4 36.6 %reduce_all.1 = (f32[3,160,320]{2,1,0:T(8,128)}, bf16[256,1280]{1,0:T(8,128)(2,1)}) custom-call(bf16[8,160,960]{2,1,0:T(8,128)(2,1)} %bitcast.9, bf16[4,256,1280]{2,1,0:T(8,128)(2,1)} %bitcast.8, bf16[256,1280]{1,0:T(8,128)(2,1)} %h_ref.1, f32[1,1280]{1,0:T(1,128)} %reshape.29.gain_ref), custom_call_target="tpu_custom_call" | custom-call | bytes 10158080 | tf_op jit(solution)/shard_map/reduce_all/pallas_call | solution.py:571
  117.0 2.0 %copy.11 = bf16[256,1280]{1,0:T(8,128)(2,1)} copy(bf16[256,1280]{1,0:T(8,128)(2,1)} %get-tuple-element.18) | data formatting | bytes 1310720
  118.9 2.0 %copy.12 = f32[160,3,320]{2,0,1:T(8,128)} copy(f32[160,3,320]{2,0,1:T(8,128)} %bitcast.13) | data formatting | bytes 1228800

commit v3 on v2

--- a/solution.py
+++ b/solution.py
@@ -37,11 +37,66 @@
     return result.astype(jnp.bfloat16)
 
 
+def part_kernel(w_ref, *out_refs):
+    first = 0
+    for out_ref in out_refs:
+        heads = out_ref.shape[1] // (3 * HD)
+        for h in range(heads):
+            for kind in range(3):
+                at = (3 * h + kind) * HD
+                source = (first + h) * HD
+                out_ref[:, at:at + HD] = w_ref[kind, :, source:source + HD]
+        first += heads
+
+
+def part_weight(weight, parts):
+    vmem = pl.BlockSpec(memory_space=pltpu.VMEM)
+    rows = weight.shape[1]
+    return pl.pallas_call(
+        part_kernel,
+        out_shape=tuple(
+            jax.ShapeDtypeStruct((rows, 3 * HD * heads), weight.dtype) for heads in parts
+        ),
+        in_specs=[vmem],
+        out_specs=(vmem,) * len(parts),
+        name="part_weight",
+    )(weight)
+
+
+def finish_kernel(wa_ref, wb_ref, h_ref, w_out, h_out):
+    first = 0
+    for ref in (wa_ref, wb_ref):
+        heads = ref.shape[1] // (3 * HD)
+        for h in range(heads):
+            for kind in range(3):
+                at = (3 * h + kind) * HD
+                target = (first + h) * HD
+                w_out[kind, :, target:target + HD] = ref[:, at:at + HD].astype(jnp.float32)
+        first += heads
+    h_out[...] = h_ref[...]
+
+
+def finish(first_grad, second_grad, hidden_grad):
+    vmem = pl.BlockSpec(memory_space=pltpu.VMEM)
+    rows = first_grad.shape[0]
+    cols = (first_grad.shape[1] + second_grad.shape[1]) // 3
+    return pl.pallas_call(
+        finish_kernel,
+        out_shape=(
+            jax.ShapeDtypeStruct((3, rows, cols), jnp.float32),
+            jax.ShapeDtypeStruct(hidden_grad.shape, hidden_grad.dtype),
+        ),
+        in_specs=[vmem] * 3,
+        out_specs=(vmem,) * 2,
+        name="finish",
+    )(first_grad, second_grad, hidden_grad)
+
+
 def gather_kernel(
-    dp, frames, w_in, h_in, gain_ref, bias_ref, t_in, wg_ref, ng_ref, tg_ref,
-    w_ref, n_ref, t_ref, w_send, w_recv, n_send, n_recv, t_send, t_recv, own_sem,
+    dp, frames, w_ref, h_in, gain_ref, bias_ref, t_in, wg_ref, ng_ref, tg_ref,
+    n_ref, t_ref, w_send, w_recv, n_send, n_recv, t_send, t_recv, own_sem,
 ):
-    head_cols = w_in.shape[2]
+    head_cols = t_in.shape[1] // frames
     line = dp // 2
     pairs = frames // 2
     i = lax.axis_index("dp")
@@ -66,11 +121,6 @@
     for step in range(1, frames):
         other = lax.rem(f + step, frames)
         pl.semaphore_signal(barrier, inc=1, device_id=(i, other), device_id_type=MESH)
-    for h in range(head_cols // HD):
-        for kind in range(3):
-            at = (3 * h + kind) * HD
-            w_ref[:, at:at + HD] = w_in[kind, :, h * HD:(h + 1) * HD]
-
     ends = jnp.where(has_right, 1, 0) + jnp.where(has_left, 1, 0)
     pl.semaphore_wait(barrier, frames + ends)
 
@@ -105,7 +155,9 @@
 
     w_copy(w_ref, i, 2, mate).start()
     sibling = u * 2 + (1 - c)
-    n_ref[...] = norm_forward(h_in[...], gain_ref[...], bias_ref[...])[0]
+    n_ref[...] = norm_forward(
+        h_in[...], gain_ref[...].reshape(1, -1), bias_ref[...].reshape(1, -1)
+    )[0]
     for step in range(1, pairs):
         far = lax.rem(u + step, pairs) * 2 + c
         n_copy(n_ref, f, step, far).start()
@@ -197,10 +249,9 @@
     any_spec = pl.BlockSpec(memory_space=pl.ANY)
     vmem = pl.BlockSpec(memory_space=pltpu.VMEM)
     pairs = frames // 2
-    kinds, own_rows, head_cols = weight.shape
     think_rows = thinker.shape[0]
-    w_own = (own_rows, kinds * head_cols)
-    t_own = (frames, think_rows, head_cols)
+    w_own = weight.shape
+    t_own = (frames, think_rows, thinker.shape[1] // frames)
     moved = 2 * (dp * weight.size + frames * hidden.size + thinker.size)
     return pl.pallas_call(
         functools.partial(gather_kernel, dp, frames),
@@ -212,7 +263,6 @@
         in_specs=[vmem] * 5,
         out_specs=(any_spec,) * 3,
         scratch_shapes=[
-            pltpu.VMEM(w_own, weight.dtype),
             pltpu.VMEM(hidden.shape, hidden.dtype),
             pltpu.VMEM(t_own, thinker.dtype),
             dma((3, dp)), dma((dp,)),
@@ -223,20 +273,23 @@
         compiler_params=pltpu.CompilerParams(
             collective_id=0, has_side_effects=True, vmem_limit_bytes=VMEM_LIMIT
         ),
-        cost_estimate=pl.CostEstimate(flops=0, bytes_accessed=2 * moved, transcendentals=0),
+        cost_estimate=pl.CostEstimate(flops=0, bytes_accessed=10 * moved, transcendentals=0),
         name="gather_all",
     )(weight, hidden, gain, bias, thinker)
 
 
-def local_kernel(
-    rows_tile, tile_q, windows, len_ref, pos_ref, n_ref, w_ref, t_ref, ng_ref, wp_ref,
-    q_s, k_s, v_s, g_s, kt_s, dq_s, dk_s, dv_s, dk_acc, dv_acc, grad_s,
-):
+def local_kernel(rows_tile, tile_q, windows, is_first, len_ref, n_ref, w_ref, *refs):
+    if is_first:
+        pos_ref, t_ref, og_ref, grad_s, wp_ref = refs[:5]
+    else:
+        og_ref, grad_a, w_a, ng_ref, wp_ref = refs[:5]
+        grad_s = refs[-1]
+    q_s, k_s, v_s, g_s, kt_s, dq_s, dk_s, dv_s, dk_acc, dv_acc = refs[5:15]
     length, width = n_ref.shape
     cols = w_ref.shape[1]
     heads = cols // (3 * HD)
+    head_from = 0 if is_first else og_ref.shape[1] // HD - heads
     recs = len_ref.shape[1]
-    slack = t_ref.shape[0] - length
     scale = HD ** (-0.5)
     expo_scale = scale * math.log2(math.e)
 
@@ -260,13 +313,17 @@
         same = seg == lane
         q_mask = jnp.where(jnp.logical_or(same, lane >= recs), 0.0, NEG).astype(jnp.bfloat16)
         k_mask = jnp.where(same, 1.0, 0.0).astype(jnp.bfloat16)
-        cover = rows_tile + slack
-        col = r0 + lax.broadcasted_iota(jnp.int32, (rows_tile, cover), 1)
-        places = jnp.broadcast_to(pos_ref[:, rows], (128, rows_tile)).T[:, 0:1]
-        pick = jnp.where(col == places, 1.0, 0.0).astype(jnp.bfloat16)
-        out_grad = jnp.dot(
-            pick, t_ref[pl.ds(r0, cover), :], preferred_element_type=jnp.float32
-        ).astype(jnp.bfloat16)
+        if is_first:
+            cover = rows_tile + t_ref.shape[0] - length
+            col = r0 + lax.broadcasted_iota(jnp.int32, (rows_tile, cover), 1)
+            places = jnp.broadcast_to(pos_ref[:, rows], (128, rows_tile)).T[:, 0:1]
+            pick = jnp.where(col == places, 1.0, 0.0).astype(jnp.bfloat16)
+            out_grad = jnp.dot(
+                pick, t_ref[pl.ds(r0, cover), :], preferred_element_type=jnp.float32
+            ).astype(jnp.bfloat16)
+            og_ref[rows, :] = out_grad
+        else:
+            out_grad = og_ref[rows, :]
         for h in range(heads):
             base = 3 * HD * h
             keys = proj[:, base + HD:base + 2 * HD]
@@ -276,7 +333,8 @@
             k_s[h, rows, HD:2 * HD] = k_mask
             kt_s[h, :, rows] = keys.T
             v_s[h, rows, :] = proj[:, base + 2 * HD:base + 3 * HD]
-            g_s[h, rows, :] = out_grad[:, h * HD:(h + 1) * HD]
+            at = (head_from + h) * HD
+            g_s[h, rows, :] = out_grad[:, at:at + HD]
 
     tiles = length // tile_q
     nt = (((1,), (1,)), ((), ()))
@@ -341,9 +399,12 @@
             parts += [dq_s[h, rows, :], dk_s[h, rows, :], dv_s[h, rows, :]]
         grad = jnp.concatenate(parts, axis=1)
         grad_s[rows, :] = grad
-        ng_ref[rows, :] = lax.dot_general(
-            grad, w_ref[...], nt, preferred_element_type=jnp.float32
-        ).astype(jnp.bfloat16)
+        if not is_first:
+            summed = lax.dot_general(grad, w_ref[...], nt, preferred_element_type=jnp.float32)
+            summed = summed + lax.dot_general(
+                grad_a[rows, :], w_a[...], nt, preferred_element_type=jnp.float32
+            )
+            ng_ref[rows, :] = summed.astype(jnp.bfloat16)
 
     @pl.loop(0, width // rows_tile)
     def _(t):
@@ -354,7 +415,7 @@
         ).astype(jnp.bfloat16)
 
 
-def local_work(lengths, positions, group_norm, weight, thinker):
+def local_work(is_first, lengths, group_norm, weight, *rest):
     length, width = group_norm.shape
     cols = weight.shape[1]
     heads = cols // (3 * HD)
@@ -363,30 +424,38 @@
     windows = tuple(w for w in (512, 768) if w < length) + (length,)
     vmem = pl.BlockSpec(memory_space=pltpu.VMEM)
     bf16, f32 = jnp.bfloat16, jnp.float32
+    grad_type = (length, cols)
+    if is_first:
+        outs = ((length, rest[1].shape[1]), grad_type, (width, cols))
+    else:
+        outs = ((length, width), (width, cols))
+    scratch = [
+        pltpu.VMEM((heads, length, 2 * HD), bf16),
+        pltpu.VMEM((heads, length, 2 * HD), bf16),
+        pltpu.VMEM((heads, length, HD), bf16),
+        pltpu.VMEM((heads, length, HD), bf16),
+        pltpu.VMEM((heads, HD, length), bf16),
+        pltpu.VMEM((heads, length, HD), bf16),
+        pltpu.VMEM((heads, length, HD), bf16),
+        pltpu.VMEM((heads, length, HD), bf16),
+        pltpu.VMEM((length, HD), f32),
+        pltpu.VMEM((length, HD), f32),
+    ]
+    if not is_first:
+        scratch.append(pltpu.VMEM(grad_type, bf16))
     return pl.pallas_call(
-        functools.partial(local_kernel, rows_tile, tile_q, windows),
-        out_shape=(
-            jax.ShapeDtypeStruct((length, width), bf16),
-            jax.ShapeDtypeStruct((width, cols), bf16),
+        functools.partial(local_kernel, rows_tile, tile_q, windows, is_first),
+        out_shape=tuple(jax.ShapeDtypeStruct(shape, bf16) for shape in outs),
+        in_specs=[pl.BlockSpec(memory_space=pltpu.SMEM)] + [vmem] * (2 + len(rest)),
+        out_specs=(vmem,) * len(outs),
+        scratch_shapes=scratch,
+        compiler_params=pltpu.CompilerParams(vmem_limit_bytes=VMEM_LIMIT),
+        cost_estimate=pl.CostEstimate(
+            flops=40 * heads * length * length * HD, bytes_accessed=4 * length * width,
+            transcendentals=heads * length * length,
         ),
-        in_specs=[pl.BlockSpec(memory_space=pltpu.SMEM)] + [vmem] * 4,
-        out_specs=(vmem, vmem),
-        scratch_shapes=[
-            pltpu.VMEM((heads, length, 2 * HD), bf16),
-            pltpu.VMEM((heads, length, 2 * HD), bf16),
-            pltpu.VMEM((heads, length, HD), bf16),
-            pltpu.VMEM((heads, length, HD), bf16),
-            pltpu.VMEM((heads, HD, length), bf16),
-            pltpu.VMEM((heads, length, HD), bf16),
-            pltpu.VMEM((heads, length, HD), bf16),
-            pltpu.VMEM((heads, length, HD), bf16),
-            pltpu.VMEM((length, HD), f32),
-            pltpu.VMEM((length, HD), f32),
-            pltpu.VMEM((length, cols), bf16),
-        ],
-        compiler_params=pltpu.CompilerParams(vmem_limit_bytes=VMEM_LIMIT),
-        name="local_work",
-    )(lengths, positions, group_norm, weight, thinker)
+        name="local_first" if is_first else "local_second",
+    )(lengths, group_norm, weight, *rest)
 
 
 def reduce_kernel(
@@ -523,10 +592,10 @@
     mean_row = jnp.mean(rows, axis=-1, keepdims=True)
     centered = rows - mean_row
     inv_std = lax.rsqrt(jnp.mean(centered * centered, axis=-1, keepdims=True) + norm_eps)
-    hout_ref[...] = norm_backward(total, centered * inv_std, inv_std, gain_ref[...])
+    gain = gain_ref[...].reshape(1, -1)
+    hout_ref[...] = norm_backward(total, centered * inv_std, inv_std, gain)
 
     pass_on(line - 1, 0)
-    kinds, _, head_cols = wout_ref.shape
     zero = jnp.zeros(wp_ref.shape[1:], f32)
 
     @pl.when(jnp.logical_not(has_left))
@@ -539,10 +608,7 @@
 
     final = wp_ref[i].astype(f32) + from_mate[p].astype(f32)
     final = final + from_line[0, p].astype(f32) + from_line[1, p].astype(f32)
-    for h in range(head_cols // HD):
-        for kind in range(kinds):
-            at = (kinds * h + kind) * HD
-            wout_ref[kind, :, h * HD:(h + 1) * HD] = final[:, at:at + HD]
+    wout_ref[...] = final
 
     def sent(q, z):
         to_mate(q).wait_send()
@@ -561,7 +627,7 @@
         to_other(v, u).wait_send()
 
 
-def reduce_all(dp, frames, weight_part, norm_part, hidden, gain, heads):
+def reduce_all(dp, frames, weight_part, norm_part, hidden, gain):
     dma = pltpu.SemaphoreType.DMA
     vmem = pl.BlockSpec(memory_space=pltpu.VMEM)
     pairs, line = frames // 2, dp // 2
@@ -571,7 +637,7 @@
     return pl.pallas_call(
         functools.partial(reduce_kernel, dp, frames),
         out_shape=(
-            jax.ShapeDtypeStruct((3, own_rows, cols // 3), f32),
+            jax.ShapeDtypeStruct((own_rows, cols), f32),
             jax.ShapeDtypeStruct(hidden.shape, bf16),
         ),
         in_specs=[vmem] * 4,
@@ -589,7 +655,7 @@
         compiler_params=pltpu.CompilerParams(
             collective_id=1, has_side_effects=True, vmem_limit_bytes=VMEM_LIMIT
         ),
-        cost_estimate=pl.CostEstimate(flops=0, bytes_accessed=2 * moved, transcendentals=0),
+        cost_estimate=pl.CostEstimate(flops=0, bytes_accessed=10 * moved, transcendentals=0),
         name="reduce_all",
     )(weight_part, norm_part, hidden, gain)
 
@@ -604,24 +670,30 @@
     own_frames, width = hidden_in.shape
     group_frames = token_positions.shape[0]
     think_rows = thinker_grad.shape[0]
-    gain = norm_gain.reshape(1, width)
-    weight, group_norm, moved = gather_all(
-        dp_count, frame_count, qkv_weight.transpose(1, 0, 2), hidden_in,
-        gain, norm_bias.reshape(1, width), thinker_grad,
+    parts = (heads // 2, heads - heads // 2)
+    first_own, second_own = part_weight(qkv_weight.transpose(1, 0, 2), parts)
+    second_weight = lax.all_gather(second_own, "dp", axis=0, tiled=True)
+    first_weight, group_norm, moved = gather_all(
+        dp_count, frame_count, first_own, hidden_in, norm_gain, norm_bias, thinker_grad
     )
-    norm_part, weight_part = local_work(
-        rec_lengths,
+    first_weight = first_weight.reshape(width, first_own.shape[1])
+    group_norm = group_norm.reshape(group_frames, width)
+    out_grad, first_grad, first_part = local_work(
+        True, rec_lengths, group_norm, first_weight,
         token_positions.reshape(1, group_frames),
-        group_norm.reshape(group_frames, width),
-        weight.reshape(width, 3 * head_cols),
         moved.reshape(frame_count * think_rows, head_cols),
     )
-    weight_grad, hidden_grad = reduce_all(
+    first_total = lax.psum_scatter(first_part, "dp", scatter_dimension=0, tiled=True)
+    norm_part, second_part = local_work(
+        False, rec_lengths, group_norm, second_weight, out_grad, first_grad, first_weight
+    )
+    second_total, hidden_grad = reduce_all(
         dp_count, frame_count,
-        weight_part.reshape(dp_count, own_rows, 3 * head_cols),
+        second_part.reshape(dp_count, own_rows, second_part.shape[1]),
         norm_part.reshape(frame_count, own_frames, width),
-        hidden_in, gain, heads,
+        hidden_in, norm_gain,
     )
+    weight_grad, hidden_grad = finish(first_total, second_total, hidden_grad)
     return (hidden_grad, weight_grad.transpose(1, 0, 2))
 
 

time: 121 us -> 136 us (1.12)
  between operations: 0.65 us -> 14.1 us
  local copies, waits for them, and re-layouts: 6.58 us -> 0 us
  Pallas kernels: 114 us -> 119 us
  waiting for transfers between devices: 0 us -> 1.96 us
    pallas_call x1, Pallas kernels: 41 us -> 32.7 us  [gather_all(): pl.pallas_call(functools.partial(gather_kernel, dp, frames), out_shape=(j...]
    pallas_call x1 -> x2, Pallas kernels: 36.1 us -> 43.5 us  [local_work(): pl.pallas_call(functools.partial(local_kernel, rows_tile, tile_q, windows...]
    pallas_call x0 -> x2, Pallas kernels: none -> 4.37 us  [the longest x1 2.53 us: finish(): pl.pallas_call(finish_kernel, out_shape=(jax.ShapeDtypeStruct((3, rows, c...]
    unnamed x2 -> x0, local copies, waits for them, and re-layouts: 3.99 us -> none
    reshape x2 -> x0, local copies, waits for them, and re-layouts: 2.59 us -> none  [the longest x1 1.29 us: per_device(): gain = norm_gain.reshape(1, width)]
    reduce_scatter x0 -> x1, waiting for transfers between devices: none -> 1.91 us  [per_device(): lax.psum_scatter(first_part, 'dp', scatter_dimension=0, tiled=True)]
    pallas_call x1, Pallas kernels: 36.6 us -> 38.1 us  [reduce_all(): pl.pallas_call(functools.partial(reduce_kernel, dp, frames), out_shape=(j...]
  transfers between devices with their start and end apart: 0 -> 2, of which waited for: 0 -> 1; matrix products, arithmetic and copies ran while one was open for 0% -> 0% of each run, Pallas kernels for 0% -> 85%
where the time goes in v3:
time: 136 us; the launch traced here: 135 us
  Pallas kernels  119 us (88%)
  between operations  14.1 us (10%)
  waiting for transfers between devices  1.96 us (1%)
    pallas_call x2, Pallas kernels, local_work(): pl.pallas_call(functools.partial(local_kernel, rows_tile, tile_q, windows...  43.5 us
    pallas_call x1, Pallas kernels, reduce_all(): pl.pallas_call(functools.partial(reduce_kernel, dp, frames), out_shape=(j...  38.1 us
    pallas_call x1, Pallas kernels, gather_all(): pl.pallas_call(functools.partial(gather_kernel, dp, frames), out_shape=(j...  32.7 us
  transfers between devices with their start and end apart: 2, of which 1 were waited for; matrix products, arithmetic and copies ran while one was open for 0% of the time, Pallas kernels for 85%

profile of v3, /device:TPU:0, one launch (start us, length us, event | category | flops | bytes accessed | tf_op | source)
XLA Modules:
  0.0 134.7 jit_solution(6005537254760329800)
XLA Ops:
  7.2 0.0 all-gather.2.cloned.1.call-start
  7.2 1.8 %part_weight.1 = (bf16[160,384]{1,0:T(8,128)(2,1)}, bf16[160,576]{1,0:T(8,128)(2,1)}) custom-call(bf16[3,160,320]{2,1,0:T(8,128)(2,1)} %bitcast.10), custom_call_target="tpu_custom_call" | custom-call | tf_op jit(solution)/shard_map/part_weight/pallas_call | solution.py:55
  9.1 0.0 all-gather.2.cloned.1.call-update
  9.1 0.0 reduce-scatter.2.cloned.1.call-start
  9.1 32.7 %gather_all.1 = (bf16[8,160,384]{2,1,0:T(8,128)(2,1)}, bf16[4,256,1280]{2,1,0:T(8,128)(2,1)}, bf16[4,384,320]{2,1,0:T(8,128)(2,1)}) custom-call(bf16[160,384]{1,0:T(8,128)(2,1)} %get-tuple-element.16.w_ref, bf16[256,1280]{1,0:T(8,128)(2,1)} %h_ref.1, f32[1280]{0:T(1024)} %gain_ref.3, f32[1280]{0:T(1024)} %bias_ref.1, bf16[384,1280]{1,0:T(8,128)(2,1)} %t_in.1), custom_call_target="tpu_custom_call" | custom-call | bytes 45875200 | tf_op jit(solution)/shard_map/gather_all/pallas_call | solution.py:256
  41.8 17.2 %local_first.1 = (bf16[1024,320]{1,0:T(8,128)(2,1)}, bf16[1024,384]{1,0:T(8,128)(2,1)}, bf16[1280,384]{1,0:T(8,128)(2,1)}) custom-call(s32[1,3]{1,0:T(1,128)} %len_ref.3, bf16[1024,1280]{1,0:T(8,128)(2,1)} %bitcast.11, bf16[1280,384]{1,0:T(8,128)(2,1)} %bitcast.14, s32[1,1024]{1,0:T(1,128)} %bitcast.17, bf16[1536,320]{1,0:T(8,128)(2,1)} %bitcast.13), custom_call_target="tpu_custom_call" | custom-call | flops 5368709120 | bytes 5242880 | tf_op jit(solution)/shard_map/local_first/pallas_call | solution.py:446
  59.0 0.0 reduce-scatter.2.cloned.1.call-update
  59.1 0.0 all-gather.2.cloned.1.call-done.w_ref
  59.1 26.2 %local_second.1 = (bf16[1024,1280]{1,0:T(8,128)(2,1)}, bf16[1280,576]{1,0:T(8,128)(2,1)}) custom-call(s32[1,3]{1,0:T(1,128)} %len_ref.3, bf16[1024,1280]{1,0:T(8,128)(2,1)} %bitcast.12, bf16[1280,576]{1,0:T(8,128)(2,1)} %all-gather.2.cloned.1.call-done.w_ref, bf16[1024,320]{1,0:T(8,128)(2,1)} %get-tuple-element.22.refs_0_, ...), custom_call_target="tpu_custom_call" | custom-call | flops 8053063680 | bytes 5242880 | tf_op jit(solution)/shard_map/local_second/pallas_call | solution.py:446
  85.3 38.1 %reduce_all.1 = (f32[160,576]{1,0:T(8,128)}, bf16[256,1280]{1,0:T(8,128)(2,1)}) custom-call(bf16[8,160,576]{2,1,0:T(8,128)(2,1)} %bitcast.9, bf16[4,256,1280]{2,1,0:T(8,128)(2,1)} %bitcast.8, bf16[256,1280]{1,0:T(8,128)(2,1)} %h_ref.1, f32[1280]{0:T(1024)} %gain_ref.3), custom_call_target="tpu_custom_call" | custom-call | bytes 40960000 | tf_op jit(solution)/shard_map/reduce_all/pallas_call | solution.py:637
  123.4 1.9 %reduce-scatter.2.cloned.1.call-done.wa_ref = bf16[160,384]{1,0:T(8,128)(2,1)} async-done(((bf16[1280,384]{1,0:T(8,128)(2,1)}), bf16[160,384]{1,0:T(8,128)(2,1)}) %reduce-scatter.2.cloned.1.call-update) | async-done | bytes 122896 | tf_op jit(solution)/shard_map/reduce_scatter | solution.py:686
  125.3 2.5 %finish.1 = (f32[3,160,320]{2,1,0:T(8,128)}, bf16[256,1280]{1,0:T(8,128)(2,1)}) custom-call(bf16[160,384]{1,0:T(8,128)(2,1)} %reduce-scatter.2.cloned.1.call-done.wa_ref, f32[160,576]{1,0:T(8,128)} %get-tuple-element.26.wb_ref, bf16[256,1280]{1,0:T(8,128)(2,1)} %get-tuple-element.27.h_ref), custom_call_target="tpu_custom_call" | custom-call | tf_op jit(solution)/shard_map/finish/pallas_call | solution.py:83
Async XLA Ops:
  7.2 51.9 %all-gather.2.cloned.1.call-start = ((), (), s32[]{:S(2)}) async-start(), calls=%async_computation.2 | async-start | bytes 1843200 | tf_op jit(solution)/shard_map/all_gather | solution.py:675
  9.1 116.2 %reduce-scatter.2.cloned.1.call-start = ((), (), s32[]{:S(2)}) async-start(), calls=%async_computation.1 | async-start | bytes 1105920 | tf_op jit(solution)/shard_map/reduce_scatter | solution.py:686
Sparse Core Ops, SparseCore 0:
  10.8 47.8 all-gather.1
  62.0 63.2 reduce-scatter.1

commit v4 on v2

--- a/solution.py
+++ b/solution.py
@@ -105,7 +105,9 @@
 
     w_copy(w_ref, i, 2, mate).start()
     sibling = u * 2 + (1 - c)
-    n_ref[...] = norm_forward(h_in[...], gain_ref[...], bias_ref[...])[0]
+    n_ref[...] = norm_forward(
+        h_in[...], gain_ref[...].reshape(1, -1), bias_ref[...].reshape(1, -1)
+    )[0]
     for step in range(1, pairs):
         far = lax.rem(u + step, pairs) * 2 + c
         n_copy(n_ref, f, step, far).start()
@@ -281,57 +283,70 @@
     tiles = length // tile_q
     nt = (((1,), (1,)), ((), ()))
 
-    @pl.loop(0, heads)
-    def _(h):
-        dk_acc[...] = jnp.zeros_like(dk_acc)
-        dv_acc[...] = jnp.zeros_like(dv_acc)
-
-        @pl.loop(0, tiles)
-        def _(t):
-            q0 = pl.multiple_of(t * tile_q, tile_q)
-            q_last = q0 + tile_q - 1
-            low = jnp.int32(0)
-            high = jnp.int32(length)
-            for end in ends:
-                low = jnp.where(end <= q0, jnp.maximum(low, end), low)
-                high = jnp.where(end > q_last, jnp.minimum(high, end), high)
-            low = (low // 128) * 128
-            need = high - low
-
-            def attend(window):
-                start = pl.multiple_of(jnp.minimum(low, length - window), 128)
-                span = pl.ds(start, window)
-                q_rows = q_s[h, pl.ds(q0, tile_q), :]
-                g_rows = g_s[h, pl.ds(q0, tile_q), :]
+    dk_acc[...] = jnp.zeros_like(dk_acc)
+    dv_acc[...] = jnp.zeros_like(dv_acc)
+
+    @pl.loop(0, tiles)
+    def _(t):
+        q0 = pl.multiple_of(t * tile_q, tile_q)
+        q_last = q0 + tile_q - 1
+        q_span = pl.ds(q0, tile_q)
+        low = jnp.int32(0)
+        high = jnp.int32(length)
+        for end in ends:
+            low = jnp.where(end <= q0, jnp.maximum(low, end), low)
+            high = jnp.where(end > q_last, jnp.minimum(high, end), high)
+        low = (low // 128) * 128
+        need = high - low
+
+        def attend(window):
+            start = pl.multiple_of(jnp.minimum(low, length - window), 128)
+            span = pl.ds(start, window)
+
+            def products(h):
                 scores = lax.dot_general(
-                    k_s[h, span, :], q_rows, nt, preferred_element_type=jnp.float32
+                    k_s[h, span, :], q_s[h, q_span, :], nt, preferred_element_type=jnp.float32
                 )
                 grads = lax.dot_general(
-                    v_s[h, span, :], g_rows, nt, preferred_element_type=jnp.float32
+                    v_s[h, span, :], g_s[h, q_span, :], nt, preferred_element_type=jnp.float32
                 )
+                return scores, grads
+
+            def softmax_grads(scores, grads):
                 top = jnp.max(scores, axis=0, keepdims=True)
                 expo = jnp.exp2((scores - top) * expo_scale)
                 weights = expo * (1.0 / jnp.sum(expo, axis=0, keepdims=True))
                 row_dot = jnp.sum(weights * grads, axis=0, keepdims=True)
                 score_grad = (weights * (grads - row_dot)).astype(jnp.bfloat16)
-                dv_acc[span, :] += jnp.dot(
-                    weights.astype(jnp.bfloat16), g_rows, preferred_element_type=jnp.float32
+                return weights.astype(jnp.bfloat16), score_grad
+
+            def accumulate(h, weights, score_grad):
+                dv_acc[h, span, :] += jnp.dot(
+                    weights, g_s[h, q_span, :], preferred_element_type=jnp.float32
                 )
-                dk_acc[span, :] += jnp.dot(
-                    score_grad, q_rows[:, 0:HD], preferred_element_type=jnp.float32
+                dk_acc[h, span, :] += jnp.dot(
+                    score_grad, q_s[h, q_span, 0:HD], preferred_element_type=jnp.float32
                 )
                 dq_t = jnp.dot(kt_s[h, :, span], score_grad, preferred_element_type=jnp.float32)
-                dq_s[h, pl.ds(q0, tile_q), :] = (dq_t * scale).T.astype(jnp.bfloat16)
-
-            smaller = 0
-            for window in windows:
-                @pl.when(jnp.logical_and(need > smaller, need <= window))
-                def _(window=window):
-                    attend(window)
-                smaller = window
-
-        dk_s[h] = (dk_acc[...] * scale).astype(jnp.bfloat16)
-        dv_s[h] = dv_acc[...].astype(jnp.bfloat16)
+                dq_s[h, q_span, :] = (dq_t * scale).T.astype(jnp.bfloat16)
+
+            ahead = products(0)
+            for h in range(heads):
+                now = ahead
+                if h + 1 < heads:
+                    ahead = products(h + 1)
+                accumulate(h, *softmax_grads(*now))
+
+        smaller = 0
+        for window in windows:
+            @pl.when(jnp.logical_and(need > smaller, need <= window))
+            def _(window=window):
+                attend(window)
+            smaller = window
+
+    for h in range(heads):
+        dk_s[h] = (dk_acc[h] * scale).astype(jnp.bfloat16)
+        dv_s[h] = dv_acc[h].astype(jnp.bfloat16)
 
     @pl.loop(0, length // rows_tile)
     def _(t):
@@ -380,8 +395,8 @@
             pltpu.VMEM((heads, length, HD), bf16),
             pltpu.VMEM((heads, length, HD), bf16),
             pltpu.VMEM((heads, length, HD), bf16),
-            pltpu.VMEM((length, HD), f32),
-            pltpu.VMEM((length, HD), f32),
+            pltpu.VMEM((heads, length, HD), f32),
+            pltpu.VMEM((heads, length, HD), f32),
             pltpu.VMEM((length, cols), bf16),
         ],
         compiler_params=pltpu.CompilerParams(vmem_limit_bytes=VMEM_LIMIT),
@@ -391,8 +406,8 @@
 
 def reduce_kernel(
     dp, frames, wp_ref, np_ref, h_ref, gain_ref, wout_ref, hout_ref,
-    from_mate, from_line, to_line, from_sib, from_far, to_far,
-    m_send, m_recv, l_send, l_recv, s_send, s_recv, f_send, f_recv,
+    own_w, own_n, from_mate, from_line, to_line, from_sib, from_far, to_far,
+    m_send, m_recv, l_send, l_recv, s_send, s_recv, f_send, f_recv, w_sem, n_sem,
 ):
     line = dp // 2
     pairs = frames // 2
@@ -406,6 +421,12 @@
     sibling = u * 2 + (1 - c)
     f32, bf16 = jnp.float32, jnp.bfloat16
 
+    def load_w(q):
+        return pltpu.make_async_copy(wp_ref.at[q * 2 + x], own_w.at[q], w_sem.at[q])
+
+    def load_n(v):
+        return pltpu.make_async_copy(np_ref.at[v * 2 + c], own_n.at[v], n_sem.at[v])
+
     barrier = pltpu.get_barrier_semaphore()
     pl.semaphore_signal(barrier, inc=1, device_id=(mate, f), device_id_type=MESH)
 
@@ -464,14 +485,20 @@
     lax.fori_loop(0, line, lambda s, z: (to_mate(target_at(s)).start(), z)[1], 0)
     to_sibling(u).start()
 
+    for v in range(pairs):
+        load_n(v).start()
+    lax.fori_loop(0, line, lambda s, z: (load_w(target_at(s)).start(), z)[1], 0)
+
     for step in range(1, pairs):
         v = lax.rem(u + step, pairs)
+        load_n(v).wait()
         to_sibling(v).wait_recv()
-        to_far[v] = (np_ref[v * 2 + c].astype(f32) + from_sib[v].astype(f32)).astype(bf16)
+        to_far[v] = (own_n[v].astype(f32) + from_sib[v].astype(f32)).astype(bf16)
         to_other(v, u).start()
 
     def pass_on(s, z):
         q = target_at(s)
+        load_w(q).wait()
         to_mate(q).wait_recv()
 
         @pl.when(jnp.logical_and(q >= p, has_left))
@@ -483,7 +510,7 @@
             along(q, 1, left).wait_recv()
 
         def own():
-            return wp_ref[q * 2 + x].astype(f32) + from_mate[q].astype(f32)
+            return own_w[q].astype(f32) + from_mate[q].astype(f32)
 
         @pl.when(q > p)
         def _():
@@ -513,8 +540,9 @@
 
     lax.fori_loop(0, line - 1, pass_on, 0)
 
+    load_n(u).wait()
     to_sibling(u).wait_recv()
-    total = np_ref[f].astype(f32) + from_sib[u].astype(f32)
+    total = own_n[u].astype(f32) + from_sib[u].astype(f32)
     for step in range(1, pairs):
         v = lax.rem(u + step, pairs)
         to_other(v, v).wait_recv()
@@ -523,10 +551,10 @@
     mean_row = jnp.mean(rows, axis=-1, keepdims=True)
     centered = rows - mean_row
     inv_std = lax.rsqrt(jnp.mean(centered * centered, axis=-1, keepdims=True) + norm_eps)
-    hout_ref[...] = norm_backward(total, centered * inv_std, inv_std, gain_ref[...])
+    gain = gain_ref[...].reshape(1, -1)
+    hout_ref[...] = norm_backward(total, centered * inv_std, inv_std, gain)
 
     pass_on(line - 1, 0)
-    kinds, _, head_cols = wout_ref.shape
     zero = jnp.zeros(wp_ref.shape[1:], f32)
 
     @pl.when(jnp.logical_not(has_left))
@@ -537,12 +565,9 @@
     def _():
         from_line[1, p] = zero.astype(bf16)
 
-    final = wp_ref[i].astype(f32) + from_mate[p].astype(f32)
+    final = own_w[p].astype(f32) + from_mate[p].astype(f32)
     final = final + from_line[0, p].astype(f32) + from_line[1, p].astype(f32)
-    for h in range(head_cols // HD):
-        for kind in range(kinds):
-            at = (kinds * h + kind) * HD
-            wout_ref[kind, :, h * HD:(h + 1) * HD] = final[:, at:at + HD]
+    wout_ref[...] = final
 
     def sent(q, z):
         to_mate(q).wait_send()
@@ -561,7 +586,7 @@
         to_other(v, u).wait_send()
 
 
-def reduce_all(dp, frames, weight_part, norm_part, hidden, gain, heads):
+def reduce_all(dp, frames, weight_part, norm_part, hidden, gain):
     dma = pltpu.SemaphoreType.DMA
     vmem = pl.BlockSpec(memory_space=pltpu.VMEM)
     pairs, line = frames // 2, dp // 2
@@ -571,12 +596,14 @@
     return pl.pallas_call(
         functools.partial(reduce_kernel, dp, frames),
         out_shape=(
-            jax.ShapeDtypeStruct((3, own_rows, cols // 3), f32),
+            jax.ShapeDtypeStruct((own_rows, cols), f32),
             jax.ShapeDtypeStruct(hidden.shape, bf16),
         ),
-        in_specs=[vmem] * 4,
+        in_specs=[pl.BlockSpec(memory_space=pl.ANY)] * 2 + [vmem] * 2,
         out_specs=(vmem,) * 2,
         scratch_shapes=[
+            pltpu.VMEM((line, own_rows, cols), bf16),
+            pltpu.VMEM((pairs,) + hidden.shape, bf16),
             pltpu.VMEM((line, own_rows, cols), bf16),
             pltpu.VMEM((2, line, own_rows, cols), bf16),
             pltpu.VMEM((line, own_rows, cols), bf16),
@@ -585,6 +612,7 @@
             pltpu.VMEM((pairs,) + hidden.shape, bf16),
             dma((line,)), dma((line,)), dma((line,)), dma((2, line)),
             dma((pairs,)), dma((pairs,)), dma((pairs,)), dma((pairs,)),
+            dma((line,)), dma((pairs,)),
         ],
         compiler_params=pltpu.CompilerParams(
             collective_id=1, has_side_effects=True, vmem_limit_bytes=VMEM_LIMIT
@@ -592,6 +620,29 @@
         cost_estimate=pl.CostEstimate(flops=0, bytes_accessed=2 * moved, transcendentals=0),
         name="reduce_all",
     )(weight_part, norm_part, hidden, gain)
+
+
+def finish_kernel(w_ref, h_ref, w_out, h_out):
+    for h in range(w_out.shape[2] // HD):
+        for kind in range(3):
+            at = (3 * h + kind) * HD
+            w_out[kind, :, h * HD:(h + 1) * HD] = w_ref[:, at:at + HD]
+    h_out[...] = h_ref[...]
+
+
+def finish(weight_grad, hidden_grad):
+    vmem = pl.BlockSpec(memory_space=pltpu.VMEM)
+    rows, cols = weight_grad.shape
+    return pl.pallas_call(
+        finish_kernel,
+        out_shape=(
+            jax.ShapeDtypeStruct((3, rows, cols // 3), jnp.float32),
+            jax.ShapeDtypeStruct(hidden_grad.shape, hidden_grad.dtype),
+        ),
+        in_specs=[vmem] * 2,
+        out_specs=(vmem,) * 2,
+        name="finish",
+    )(weight_grad, hidden_grad)
 
 
 def per_device(
@@ -604,10 +655,9 @@
     own_frames, width = hidden_in.shape
     group_frames = token_positions.shape[0]
     think_rows = thinker_grad.shape[0]
-    gain = norm_gain.reshape(1, width)
     weight, group_norm, moved = gather_all(
         dp_count, frame_count, qkv_weight.transpose(1, 0, 2), hidden_in,
-        gain, norm_bias.reshape(1, width), thinker_grad,
+        norm_gain, norm_bias, thinker_grad,
     )
     norm_part, weight_part = local_work(
         rec_lengths,
@@ -616,12 +666,13 @@
         weight.reshape(width, 3 * head_cols),
         moved.reshape(frame_count * think_rows, head_cols),
     )
-    weight_grad, hidden_grad = reduce_all(
+    weight_total, hidden_grad = reduce_all(
         dp_count, frame_count,
         weight_part.reshape(dp_count, own_rows, 3 * head_cols),
         norm_part.reshape(frame_count, own_frames, width),
-        hidden_in, gain, heads,
+        hidden_in, norm_gain,
     )
+    weight_grad, hidden_grad = finish(weight_total, hidden_grad)
     return (hidden_grad, weight_grad.transpose(1, 0, 2))
 
 

time: 121 us -> 112 us (0.926); the launches traced: 121 us -> 111 us
  local copies, waits for them, and re-layouts: 6.58 us -> 0 us
  Pallas kernels: 114 us -> 110 us
    pallas_call x1, Pallas kernels: 36.1 us -> 27.5 us  [local_work(): pl.pallas_call(functools.partial(local_kernel, rows_tile, tile_q, windows...]
    unnamed x2 -> x0, local copies, waits for them, and re-layouts: 3.99 us -> none
    reshape x2 -> x0, local copies, waits for them, and re-layouts: 2.59 us -> none  [the longest x1 1.29 us: per_device(): gain = norm_gain.reshape(1, width)]
    pallas_call x0 -> x1, Pallas kernels: none -> 2.54 us  [finish(): pl.pallas_call(finish_kernel, out_shape=(jax.ShapeDtypeStruct((3, rows, c...]
    pallas_call x1, Pallas kernels: 36.6 us -> 38.9 us  [reduce_all(): pl.pallas_call(functools.partial(reduce_kernel, dp, frames), out_shape=(j...]
where the time goes in v4:
time: 112 us; the launch traced here: 111 us
  Pallas kernels  110 us (98%)
    pallas_call x1, Pallas kernels, gather_all(): pl.pallas_call(functools.partial(gather_kernel, dp, frames), out_shape=(j...  41 us
    pallas_call x1, Pallas kernels, reduce_all(): pl.pallas_call(functools.partial(reduce_kernel, dp, frames), out_shape=(j...  38.9 us
    pallas_call x1, Pallas kernels, local_work(): pl.pallas_call(functools.partial(local_kernel, rows_tile, tile_q, windows...  27.5 us
    pallas_call x1, Pallas kernels, finish(): pl.pallas_call(finish_kernel, out_shape=(jax.ShapeDtypeStruct((3, rows, c...  2.54 us

profile of v4, /device:TPU:0, one launch (start us, length us, event | category | flops | bytes accessed | tf_op | source)
XLA Modules:
  0.0 110.7 jit_solution(13671522998877876430)
XLA Ops:
  0.6 41.0 %gather_all.1 = (bf16[8,160,960]{2,1,0:T(8,128)(2,1)}, bf16[4,256,1280]{2,1,0:T(8,128)(2,1)}, bf16[4,384,320]{2,1,0:T(8,128)(2,1)}) custom-call(bf16[3,160,320]{2,1,0:T(8,128)(2,1)} %bitcast.13, bf16[256,1280]{1,0:T(8,128)(2,1)} %h_ref.1, f32[1280]{0:T(1024)} %gain_ref.3, f32[1280]{0:T(1024)} %bias_ref.1, bf16[384,1280]{1,0:T(8,128)(2,1)} %t_in.1), custom_call_target="tpu_custom_call" | custom-call | bytes 12124160 | tf_op jit(solution)/shard_map/gather_all/pallas_call | solution.py:207
  41.7 27.5 %local_work.1 = (bf16[1024,1280]{1,0:T(8,128)(2,1)}, bf16[1280,960]{1,0:T(8,128)(2,1)}) custom-call(s32[1,3]{1,0:T(1,128)} %len_ref.1, s32[1,1024]{1,0:T(1,128)} %bitcast.14, bf16[1024,1280]{1,0:T(8,128)(2,1)} %bitcast.11, bf16[1280,960]{1,0:T(8,128)(2,1)} %bitcast.10, bf16[1536,320]{1,0:T(8,128)(2,1)} %bitcast.12), custom_call_target="tpu_custom_call" | custom-call | tf_op jit(solution)/shard_map/local_work/pallas_call | solution.py:381
  69.2 38.9 %reduce_all.1 = (f32[160,960]{1,0:T(8,128)}, bf16[256,1280]{1,0:T(8,128)(2,1)}) custom-call(bf16[8,160,960]{2,1,0:T(8,128)(2,1)} %bitcast.9, bf16[4,256,1280]{2,1,0:T(8,128)(2,1)} %bitcast.8, bf16[256,1280]{1,0:T(8,128)(2,1)} %h_ref.1, f32[1280]{0:T(1024)} %gain_ref.3), custom_call_target="tpu_custom_call" | custom-call | bytes 10158080 | tf_op jit(solution)/shard_map/reduce_all/pallas_call | solution.py:596
  108.2 2.5 %finish.1 = (f32[3,160,320]{2,1,0:T(8,128)}, bf16[256,1280]{1,0:T(8,128)(2,1)}) custom-call(f32[160,960]{1,0:T(8,128)} %get-tuple-element.16.w_ref, bf16[256,1280]{1,0:T(8,128)(2,1)} %get-tuple-element.17.h_ref), custom_call_target="tpu_custom_call" | custom-call | tf_op jit(solution)/shard_map/finish/pallas_call | solution.py:636

commit v5 on v4

--- a/solution.py
+++ b/solution.py
@@ -231,8 +231,8 @@
 
 
 def local_kernel(
-    rows_tile, tile_q, windows, len_ref, pos_ref, n_ref, w_ref, t_ref, ng_ref, wp_ref,
-    q_s, k_s, v_s, g_s, kt_s, dq_s, dk_s, dv_s, dk_acc, dv_acc, grad_s,
+    rows_tile, tile_q, windows, len_ref, pos_ref, n_ref, w_ref, t_ref, grad_s, nt_ref,
+    q_s, k_s, v_s, g_s, kt_s, dq_s, dk_s, dv_s, dk_acc, dv_acc,
 ):
     length, width = n_ref.shape
     cols = w_ref.shape[1]
@@ -330,6 +330,7 @@
                 dq_t = jnp.dot(kt_s[h, :, span], score_grad, preferred_element_type=jnp.float32)
                 dq_s[h, q_span, :] = (dq_t * scale).T.astype(jnp.bfloat16)
 
+            nt_ref[:, q_span] = n_ref[q_span, :].T
             ahead = products(0)
             for h in range(heads):
                 now = ahead
@@ -356,17 +357,6 @@
             parts += [dq_s[h, rows, :], dk_s[h, rows, :], dv_s[h, rows, :]]
         grad = jnp.concatenate(parts, axis=1)
         grad_s[rows, :] = grad
-        ng_ref[rows, :] = lax.dot_general(
-            grad, w_ref[...], nt, preferred_element_type=jnp.float32
-        ).astype(jnp.bfloat16)
-
-    @pl.loop(0, width // rows_tile)
-    def _(t):
-        rows = pl.ds(pl.multiple_of(t * rows_tile, rows_tile), rows_tile)
-        wp_ref[rows, :] = lax.dot_general(
-            n_ref[:, rows], grad_s[...], (((0,), (0,)), ((), ())),
-            preferred_element_type=jnp.float32,
-        ).astype(jnp.bfloat16)
 
 
 def local_work(lengths, positions, group_norm, weight, thinker):
@@ -381,8 +371,8 @@
     return pl.pallas_call(
         functools.partial(local_kernel, rows_tile, tile_q, windows),
         out_shape=(
-            jax.ShapeDtypeStruct((length, width), bf16),
-            jax.ShapeDtypeStruct((width, cols), bf16),
+            jax.ShapeDtypeStruct((length, cols), bf16),
+            jax.ShapeDtypeStruct((width, length), bf16),
         ),
         in_specs=[pl.BlockSpec(memory_space=pltpu.SMEM)] + [vmem] * 4,
         out_specs=(vmem, vmem),
@@ -397,7 +387,6 @@
             pltpu.VMEM((heads, length, HD), bf16),
             pltpu.VMEM((heads, length, HD), f32),
             pltpu.VMEM((heads, length, HD), f32),
-            pltpu.VMEM((length, cols), bf16),
         ],
         compiler_params=pltpu.CompilerParams(vmem_limit_bytes=VMEM_LIMIT),
         name="local_work",
@@ -405,9 +394,9 @@
 
 
 def reduce_kernel(
-    dp, frames, wp_ref, np_ref, h_ref, gain_ref, wout_ref, hout_ref,
-    own_w, own_n, from_mate, from_line, to_line, from_sib, from_far, to_far,
-    m_send, m_recv, l_send, l_recv, s_send, s_recv, f_send, f_recv, w_sem, n_sem,
+    dp, frames, nt_ref, grad_ref, w_hbm, h_ref, gain_ref, wout_ref, hout_ref,
+    w_ref, wp_ref, np_ref, own_w, own_n, from_mate, from_line, to_line, from_sib, from_far, to_far,
+    m_send, m_recv, l_send, l_recv, s_send, s_recv, f_send, f_recv, w_sem,
 ):
     line = dp // 2
     pairs = frames // 2
@@ -420,12 +409,19 @@
     has_right, has_left = p < line - 1, p > 0
     sibling = u * 2 + (1 - c)
     f32, bf16 = jnp.float32, jnp.bfloat16
-
-    def load_w(q):
-        return pltpu.make_async_copy(wp_ref.at[q * 2 + x], own_w.at[q], w_sem.at[q])
-
-    def load_n(v):
-        return pltpu.make_async_copy(np_ref.at[v * 2 + c], own_n.at[v], n_sem.at[v])
+    own_frames = h_ref.shape[0]
+
+    load = pltpu.make_async_copy(w_hbm, w_ref, w_sem)
+    load.start()
+
+    def weight_block(slot):
+        return jnp.dot(nt_ref[slot], grad_ref[...], preferred_element_type=f32).astype(bf16)
+
+    def norm_block(owner):
+        rows = pl.ds(pl.multiple_of(owner * own_frames, own_frames), own_frames)
+        return lax.dot_general(
+            grad_ref[rows, :], w_ref[...], (((1,), (1,)), ((), ())), preferred_element_type=f32
+        ).astype(bf16)
 
     barrier = pltpu.get_barrier_semaphore()
     pl.semaphore_signal(barrier, inc=1, device_id=(mate, f), device_id_type=MESH)
@@ -447,7 +443,7 @@
 
     def to_mate(q):
         return pltpu.make_async_remote_copy(
-            src_ref=wp_ref.at[q * 2 + (1 - x)], dst_ref=from_mate.at[q],
+            src_ref=wp_ref.at[q], dst_ref=from_mate.at[q],
             send_sem=m_send.at[q], recv_sem=m_recv.at[q],
             device_id=(mate, f), device_id_type=MESH,
         )
@@ -461,7 +457,7 @@
 
     def to_sibling(v):
         return pltpu.make_async_remote_copy(
-            src_ref=np_ref.at[v * 2 + (1 - c)], dst_ref=from_sib.at[v],
+            src_ref=np_ref.at[v], dst_ref=from_sib.at[v],
             send_sem=s_send.at[v], recv_sem=s_recv.at[v],
             device_id=(i, sibling), device_id_type=MESH,
         )
@@ -480,25 +476,34 @@
         upper = jnp.where(s < behind, s, line - 1 - (s - behind))
         return jnp.where(p < line // 2, lower, upper)
 
+    def send_block(s, z):
+        q = target_at(s)
+        wp_ref[q] = weight_block(q * 2 + (1 - x))
+        to_mate(q).start()
+        return z
+
+    def send_norm(v):
+        np_ref[v] = norm_block(v * 2 + (1 - c))
+        to_sibling(v).start()
+
+    send_block(0, 0)
+    load.wait()
     for step in range(1, pairs):
-        to_sibling(lax.rem(u + step, pairs)).start()
-    lax.fori_loop(0, line, lambda s, z: (to_mate(target_at(s)).start(), z)[1], 0)
-    to_sibling(u).start()
-
+        send_norm(lax.rem(u + step, pairs))
+    lax.fori_loop(1, line, send_block, 0)
+    send_norm(u)
     for v in range(pairs):
-        load_n(v).start()
-    lax.fori_loop(0, line, lambda s, z: (load_w(target_at(s)).start(), z)[1], 0)
+        own_n[v] = norm_block(v * 2 + c)
 
     for step in range(1, pairs):
         v = lax.rem(u + step, pairs)
-        load_n(v).wait()
         to_sibling(v).wait_recv()
         to_far[v] = (own_n[v].astype(f32) + from_sib[v].astype(f32)).astype(bf16)
         to_other(v, u).start()
 
     def pass_on(s, z):
         q = target_at(s)
-        load_w(q).wait()
+        own_w[q] = weight_block(q * 2 + x)
         to_mate(q).wait_recv()
 
         @pl.when(jnp.logical_and(q >= p, has_left))
@@ -540,7 +545,6 @@
 
     lax.fori_loop(0, line - 1, pass_on, 0)
 
-    load_n(u).wait()
     to_sibling(u).wait_recv()
     total = own_n[u].astype(f32) + from_sib[u].astype(f32)
     for step in range(1, pairs):
@@ -586,22 +590,25 @@
         to_other(v, u).wait_send()
 
 
-def reduce_all(dp, frames, weight_part, norm_part, hidden, gain):
+def reduce_all(dp, frames, norm_t, grad, weight, hidden, gain):
     dma = pltpu.SemaphoreType.DMA
     vmem = pl.BlockSpec(memory_space=pltpu.VMEM)
     pairs, line = frames // 2, dp // 2
     bf16, f32 = jnp.bfloat16, jnp.float32
-    own_rows, cols = weight_part.shape[1:]
-    moved = 2 * (weight_part.size + norm_part.size)
+    own_rows, cols = norm_t.shape[1], grad.shape[1]
+    moved = 2 * (norm_t.size + weight.size)
     return pl.pallas_call(
         functools.partial(reduce_kernel, dp, frames),
         out_shape=(
             jax.ShapeDtypeStruct((own_rows, cols), f32),
             jax.ShapeDtypeStruct(hidden.shape, bf16),
         ),
-        in_specs=[pl.BlockSpec(memory_space=pl.ANY)] * 2 + [vmem] * 2,
+        in_specs=[vmem] * 2 + [pl.BlockSpec(memory_space=pl.ANY)] + [vmem] * 2,
         out_specs=(vmem,) * 2,
         scratch_shapes=[
+            pltpu.VMEM(weight.shape, bf16),
+            pltpu.VMEM((line, own_rows, cols), bf16),
+            pltpu.VMEM((pairs,) + hidden.shape, bf16),
             pltpu.VMEM((line, own_rows, cols), bf16),
             pltpu.VMEM((pairs,) + hidden.shape, bf16),
             pltpu.VMEM((line, own_rows, cols), bf16),
@@ -612,14 +619,14 @@
             pltpu.VMEM((pairs,) + hidden.shape, bf16),
             dma((line,)), dma((line,)), dma((line,)), dma((2, line)),
             dma((pairs,)), dma((pairs,)), dma((pairs,)), dma((pairs,)),
-            dma((line,)), dma((pairs,)),
+            dma,
         ],
         compiler_params=pltpu.CompilerParams(
             collective_id=1, has_side_effects=True, vmem_limit_bytes=VMEM_LIMIT
         ),
         cost_estimate=pl.CostEstimate(flops=0, bytes_accessed=2 * moved, transcendentals=0),
         name="reduce_all",
-    )(weight_part, norm_part, hidden, gain)
+    )(norm_t, grad, weight, hidden, gain)
 
 
 def finish_kernel(w_ref, h_ref, w_out, h_out):
@@ -659,17 +666,17 @@
         dp_count, frame_count, qkv_weight.transpose(1, 0, 2), hidden_in,
         norm_gain, norm_bias, thinker_grad,
     )
-    norm_part, weight_part = local_work(
+    weight = weight.reshape(width, 3 * head_cols)
+    grad, norm_t = local_work(
         rec_lengths,
         token_positions.reshape(1, group_frames),
         group_norm.reshape(group_frames, width),
-        weight.reshape(width, 3 * head_cols),
+        weight,
         moved.reshape(frame_count * think_rows, head_cols),
     )
     weight_total, hidden_grad = reduce_all(
         dp_count, frame_count,
-        weight_part.reshape(dp_count, own_rows, 3 * head_cols),
-        norm_part.reshape(frame_count, own_frames, width),
+        norm_t.reshape(dp_count, own_rows, group_frames), grad, weight,
         hidden_in, norm_gain,
     )
     weight_grad, hidden_grad = finish(weight_total, hidden_grad)

time: 112 us -> 109 us (0.973)
  Pallas kernels: 110 us -> 108 us
    pallas_call x1, Pallas kernels: 27.5 us -> 21.9 us  [local_work(): pl.pallas_call(functools.partial(local_kernel, rows_tile, tile_q, windows...]
    pallas_call x1, Pallas kernels: 38.9 us -> 42.6 us  [reduce_all(): pl.pallas_call(functools.partial(reduce_kernel, dp, frames), out_shape=(j...]
where the time goes in v5:
time: 109 us
  Pallas kernels  108 us (99%)
    pallas_call x1, Pallas kernels, reduce_all(): pl.pallas_call(functools.partial(reduce_kernel, dp, frames), out_shape=(j...  42.6 us
    pallas_call x1, Pallas kernels, gather_all(): pl.pallas_call(functools.partial(gather_kernel, dp, frames), out_shape=(j...  41 us
    pallas_call x1, Pallas kernels, local_work(): pl.pallas_call(functools.partial(local_kernel, rows_tile, tile_q, windows...  21.9 us
    pallas_call x1, Pallas kernels, finish(): pl.pallas_call(finish_kernel, out_shape=(jax.ShapeDtypeStruct((3, rows, c...  2.54 us

profile of v5, /device:TPU:0, one launch (start us, length us, event | category | flops | bytes accessed | tf_op | source)
XLA Modules:
  0.0 108.8 jit_solution(2667421275136153302)
XLA Ops:
  0.6 41.0 %gather_all.1 = (bf16[8,160,960]{2,1,0:T(8,128)(2,1)}, bf16[4,256,1280]{2,1,0:T(8,128)(2,1)}, bf16[4,384,320]{2,1,0:T(8,128)(2,1)}) custom-call(bf16[3,160,320]{2,1,0:T(8,128)(2,1)} %bitcast.12, bf16[256,1280]{1,0:T(8,128)(2,1)} %h_ref.1, f32[1280]{0:T(1024)} %gain_ref.3, f32[1280]{0:T(1024)} %bias_ref.1, bf16[384,1280]{1,0:T(8,128)(2,1)} %t_in.1), custom_call_target="tpu_custom_call" | custom-call | bytes 12124160 | tf_op jit(solution)/shard_map/gather_all/pallas_call | solution.py:207
  41.7 21.9 %local_work.1 = (bf16[1024,960]{1,0:T(8,128)(2,1)}, bf16[1280,1024]{1,0:T(8,128)(2,1)}) custom-call(s32[1,3]{1,0:T(1,128)} %len_ref.1, s32[1,1024]{1,0:T(1,128)} %bitcast.13, bf16[1024,1280]{1,0:T(8,128)(2,1)} %bitcast.10, bf16[1280,960]{1,0:T(8,128)(2,1)} %bitcast.7, bf16[1536,320]{1,0:T(8,128)(2,1)} %bitcast.11), custom_call_target="tpu_custom_call" | custom-call | tf_op jit(solution)/shard_map/local_work/pallas_call | solution.py:371
  63.6 42.6 %reduce_all.1 = (f32[160,960]{1,0:T(8,128)}, bf16[256,1280]{1,0:T(8,128)(2,1)}) custom-call(bf16[8,160,1024]{2,1,0:T(8,128)(2,1)} %bitcast.9, bf16[1024,960]{1,0:T(8,128)(2,1)} %get-tuple-element.15.grad_ref, bf16[1280,960]{1,0:T(8,128)(2,1)} %bitcast.8, bf16[256,1280]{1,0:T(8,128)(2,1)} %h_ref.1, f32[1280]{0:T(1024)} %gain_ref.3), custom_call_target="tpu_custom_call" | custom-call | bytes 10158080 | tf_op jit(solution)/shard_map/reduce_all/pallas_call | solution.py:600
  106.2 2.5 %finish.1 = (f32[3,160,320]{2,1,0:T(8,128)}, bf16[256,1280]{1,0:T(8,128)(2,1)}) custom-call(f32[160,960]{1,0:T(8,128)} %get-tuple-element.16.w_ref, bf16[256,1280]{1,0:T(8,128)(2,1)} %get-tuple-element.17.h_ref), custom_call_target="tpu_custom_call" | custom-call | tf_op jit(solution)/shard_map/finish/pallas_call | solution.py:643

commit v6 on v5

--- a/solution.py
+++ b/solution.py
@@ -38,10 +38,15 @@
 
 
 def gather_kernel(
-    dp, frames, w_in, h_in, gain_ref, bias_ref, t_in, wg_ref, ng_ref, tg_ref,
-    w_ref, n_ref, t_ref, w_send, w_recv, n_send, n_recv, t_send, t_recv, own_sem,
+    dp, frames, w_in, h_hbm, gain_ref, bias_ref, t_hbm, wg_ref, ng_ref, tg_ref,
+    h_in, t_in, w_ref, n_ref, t_ref,
+    w_send, w_recv, n_send, n_recv, t_send, t_recv, own_sem, in_sem,
 ):
     head_cols = w_in.shape[2]
+    load_h = pltpu.make_async_copy(h_hbm, h_in, in_sem.at[0])
+    load_t = pltpu.make_async_copy(t_hbm, t_in, in_sem.at[1])
+    load_h.start()
+    load_t.start()
     line = dp // 2
     pairs = frames // 2
     i = lax.axis_index("dp")
@@ -105,6 +110,7 @@
 
     w_copy(w_ref, i, 2, mate).start()
     sibling = u * 2 + (1 - c)
+    load_h.wait()
     n_ref[...] = norm_forward(
         h_in[...], gain_ref[...].reshape(1, -1), bias_ref[...].reshape(1, -1)
     )[0]
@@ -112,6 +118,7 @@
         far = lax.rem(u + step, pairs) * 2 + c
         n_copy(n_ref, f, step, far).start()
     n_copy(n_ref, f, 0, sibling).start()
+    load_t.wait()
     for target in range(frames):
         t_ref[target] = t_in[:, target * head_cols:(target + 1) * head_cols]
     for step in range(1, frames):
@@ -211,16 +218,18 @@
             jax.ShapeDtypeStruct((frames,) + hidden.shape, hidden.dtype),
             jax.ShapeDtypeStruct(t_own, thinker.dtype),
         ),
-        in_specs=[vmem] * 5,
+        in_specs=[vmem, any_spec, vmem, vmem, any_spec],
         out_specs=(any_spec,) * 3,
         scratch_shapes=[
+            pltpu.VMEM(hidden.shape, hidden.dtype),
+            pltpu.VMEM(thinker.shape, thinker.dtype),
             pltpu.VMEM(w_own, weight.dtype),
             pltpu.VMEM(hidden.shape, hidden.dtype),
             pltpu.VMEM(t_own, thinker.dtype),
             dma((3, dp)), dma((dp,)),
             dma((pairs, frames)), dma((frames,)),
             dma((frames,)), dma((frames,)),
-            dma((3,)),
+            dma((3,)), dma((2,)),
         ],
         compiler_params=pltpu.CompilerParams(
             collective_id=0, has_side_effects=True, vmem_limit_bytes=VMEM_LIMIT
@@ -365,7 +374,7 @@
     heads = cols // (3 * HD)
     rows_tile = 256
     tile_q = 256
-    windows = tuple(w for w in (512, 768) if w < length) + (length,)
+    windows = tuple(w for w in (512, 640, 768, 896) if w < length) + (length,)
     vmem = pl.BlockSpec(memory_space=pltpu.VMEM)
     bf16, f32 = jnp.bfloat16, jnp.float32
     return pl.pallas_call(

time: 109 us -> 103 us (0.945)
  Pallas kernels: 108 us -> 102 us
    pallas_call x1, Pallas kernels: 42.6 us -> 36.6 us  [reduce_all(): pl.pallas_call(functools.partial(reduce_kernel, dp, frames), out_shape=(j...]
where the time goes in v6:
time: 103 us; the launch traced here: 102 us
  Pallas kernels  102 us (99%)
    pallas_call x1, Pallas kernels, gather_all(): pl.pallas_call(functools.partial(gather_kernel, dp, frames), out_shape=(j...  40.5 us
    pallas_call x1, Pallas kernels, reduce_all(): pl.pallas_call(functools.partial(reduce_kernel, dp, frames), out_shape=(j...  36.6 us
    pallas_call x1, Pallas kernels, local_work(): pl.pallas_call(functools.partial(local_kernel, rows_tile, tile_q, windows...  22.2 us
    pallas_call x1, Pallas kernels, finish(): pl.pallas_call(finish_kernel, out_shape=(jax.ShapeDtypeStruct((3, rows, c...  2.54 us

profile of v6, /device:TPU:0, one launch (start us, length us, event | category | flops | bytes accessed | tf_op | source)
XLA Modules:
  0.0 102.4 jit_solution(1539254471086271649)
XLA Ops:
  0.6 40.5 %gather_all.1 = (bf16[8,160,960]{2,1,0:T(8,128)(2,1)}, bf16[4,256,1280]{2,1,0:T(8,128)(2,1)}, bf16[4,384,320]{2,1,0:T(8,128)(2,1)}) custom-call(bf16[3,160,320]{2,1,0:T(8,128)(2,1)} %bitcast.12, bf16[256,1280]{1,0:T(8,128)(2,1)} %h_ref.1, f32[1280]{0:T(1024)} %gain_ref.3, f32[1280]{0:T(1024)} %bias_ref.1, bf16[384,1280]{1,0:T(8,128)(2,1)} %t_hbm.1), custom_call_target="tpu_custom_call" | custom-call | bytes 12124160 | tf_op jit(solution)/shard_map/gather_all/pallas_call | solution.py:214
  41.2 22.2 %local_work.1 = (bf16[1024,960]{1,0:T(8,128)(2,1)}, bf16[1280,1024]{1,0:T(8,128)(2,1)}) custom-call(s32[1,3]{1,0:T(1,128)} %len_ref.1, s32[1,1024]{1,0:T(1,128)} %bitcast.13, bf16[1024,1280]{1,0:T(8,128)(2,1)} %bitcast.10, bf16[1280,960]{1,0:T(8,128)(2,1)} %bitcast.7, bf16[1536,320]{1,0:T(8,128)(2,1)} %bitcast.11), custom_call_target="tpu_custom_call" | custom-call | tf_op jit(solution)/shard_map/local_work/pallas_call | solution.py:380
  63.3 36.6 %reduce_all.1 = (f32[160,960]{1,0:T(8,128)}, bf16[256,1280]{1,0:T(8,128)(2,1)}) custom-call(bf16[8,160,1024]{2,1,0:T(8,128)(2,1)} %bitcast.9, bf16[1024,960]{1,0:T(8,128)(2,1)} %get-tuple-element.15.grad_ref, bf16[1280,960]{1,0:T(8,128)(2,1)} %bitcast.8, bf16[256,1280]{1,0:T(8,128)(2,1)} %h_ref.1, f32[1280]{0:T(1024)} %gain_ref.3), custom_call_target="tpu_custom_call" | custom-call | bytes 10158080 | tf_op jit(solution)/shard_map/reduce_all/pallas_call | solution.py:609
  99.9 2.5 %finish.1 = (f32[3,160,320]{2,1,0:T(8,128)}, bf16[256,1280]{1,0:T(8,128)(2,1)}) custom-call(f32[160,960]{1,0:T(8,128)} %get-tuple-element.16.w_ref, bf16[256,1280]{1,0:T(8,128)(2,1)} %get-tuple-element.17.h_ref), custom_call_target="tpu_custom_call" | custom-call | tf_op jit(solution)/shard_map/finish/pallas_call | solution.py:652
